TPU v7x, 32 devices: a whole 2x2x4 slice. The times are simulated.
32 devices in a mesh: dp: 2 (over core), wide: 8 (over z, y), narrow: 2 (over x).
Axes of the slice: x: 2, y: 2, z: 4, core: 2. Of those that a mesh axis runs over, the one named last changes fastest.
Arguments:
- enc_input: bfloat16 [16384, 768], P(('dp', 'wide', 'narrow')), may hold values from -6 to 6
- dec_input: bfloat16 [4096, 768], P(('dp', 'wide', 'narrow')), may hold values from -6 to 6
- enc_lengths: int32 [16, 4], P(('dp', 'wide')), may hold values from 1 to 512, 1024 in all within a row
- dec_lengths: int32 [16, 4], P(('dp', 'wide')), may hold values from 1 to 128, 256 in all within a row
- attn_query: bfloat16 [3, 768, 768], P(None, 'wide', 'narrow'), may hold values from -0.0546875 to 0.0546875
- attn_kv: bfloat16 [3, 2, 768, 768], P(None, None, 'wide', 'narrow'), may hold values from -0.21875 to 0.21875
- attn_out: bfloat16 [3, 768, 768], P(None, 'narrow', 'wide'), may hold values from -0.875 to 0.875
- ffn_up: bfloat16 [2, 768, 3072], P(None, 'wide', 'narrow'), may hold values from -0.21875 to 0.21875
- ffn_down: bfloat16 [2, 3072, 768], P(None, 'narrow', 'wide'), may hold values from -0.109375 to 0.109375
- gains: bfloat16 [6, 768], replicated, may hold values from 0.5 to 1.5
- rel_bias: bfloat16 [2, 32, 12], P(None, None, 'narrow'), may hold values from -4 to 4
- enc_cotangent: bfloat16 [16384, 768], P(('dp', 'wide', 'narrow')), may hold values from -6 to 6
- dec_cotangent: bfloat16 [4096, 768], P(('dp', 'wide', 'narrow')), may hold values from -6 to 6
Outputs:
- enc_output: bfloat16 [16384, 768], P(('dp', 'wide', 'narrow'))
- dec_output: bfloat16 [4096, 768], P(('dp', 'wide', 'narrow'))
- enc_grad: float32 [16384, 768], P(('dp', 'wide', 'narrow'))
- dec_grad: float32 [4096, 768], P(('dp', 'wide', 'narrow'))
- grad_query: float32 [3, 768, 768], P(None, 'wide', 'narrow')
- grad_kv: float32 [3, 2, 768, 768], P(None, None, 'wide', 'narrow')
- grad_out: float32 [3, 768, 768], P(None, 'narrow', 'wide')
- grad_up: float32 [2, 768, 3072], P(None, 'wide', 'narrow')
- grad_down: float32 [2, 3072, 768], P(None, 'narrow', 'wide')
- grad_gains: float32 [6, 768], replicated
- grad_bias: float32 [2, 32, 12], P(None, None, 'narrow')
Inputs may be any that keep to these rules, and one draw needn't show every extreme that they name: `enc_lengths`: each row lists the lengths of 4 packed documents in order; they sum to 1024, and the longest is 512. `dec_lengths`: each row lists the decoder lengths of the same 4 documents in order; they sum to 256, and the longest is 128.
All inputs are finite; a program needn't handle non-finite values.
Results may differ from a plain program's by a relative error of at most 0.028.
Values may be sent and summed in bfloat16 or wider, within the bound.
A program may use at most 256 MiB of HBM per device.

v0:
```python
import functools
import math

import jax
import jax.numpy as jnp
from jax import lax
from jax.sharding import PartitionSpec as P
import jax.experimental.pallas as pl
import jax.experimental.pallas.tpu as pltpu

H = 12
DK = 64
NB = 32
MAXD = 128
ENC = 1024
DEC = 256


EPS = 1e-06
NEG = -1e30
HIGH = lax.Precision.HIGHEST
VMEM_BYTES = 56 * 2**20


def cutoffs(exact, buckets):
    found = []
    reach = exact
    for target in range(exact + 1, buckets):
        while (
            exact + math.floor(math.log(reach / exact) / math.log(MAXD / exact) * (buckets - exact))
            < target
        ):
            reach = reach + 1
        found.append(reach)
    return found


def bucket_index(relative, two_sided):
    if two_sided:
        width = NB // 2
        offset = jnp.where(relative > 0, width, 0)
        distance = jnp.abs(relative)
    else:
        width = NB
        offset = jnp.zeros_like(relative)
        distance = jnp.maximum(-relative, 0)
    exact = width // 2
    beyond = exact + sum(((distance >= limit).astype(jnp.int32) for limit in cutoffs(exact, width)))
    return offset + jnp.where(distance < exact, distance, beyond)


def segment_ids(lengths, count):
    bounds = jnp.cumsum(lengths)
    places = jnp.arange(count, dtype=jnp.int32)
    return jnp.sum((places[:, None] >= bounds[None, :]).astype(jnp.int32), axis=1)


def rms_norm(values, gain):
    return values * lax.rsqrt(jnp.mean(values * values, axis=-1, keepdims=True) + EPS) * gain


def gelu_tanh(values):
    return jax.nn.gelu(values, approximate=True)


PAIR = 128


def offset_buckets(span, two_sided):
    places = jnp.arange(2 * span, dtype=jnp.int32)[None, :]
    relative = lax.rem(places - jnp.arange(8, dtype=jnp.int32)[:, None] + 2 * span, 2 * span) - span
    buckets = bucket_index(relative.reshape(-1), two_sided)
    return (buckets[None, :] == jnp.arange(NB, dtype=jnp.int32)[:, None]).astype(jnp.bfloat16)


def base_rows(table, span, two_sided):
    heads = table.shape[1]
    rows = lax.dot_general(
        table, offset_buckets(span, two_sided), (((0,), (0,)), ((), ())), preferred_element_type=jnp.float32
    )
    return rows.reshape(heads // 2, 2, 8, 2 * span)


def table_grad(offset_sums, span, two_sided):
    heads = 2 * offset_sums.shape[0]
    return lax.dot_general(
        offset_buckets(span, two_sided).astype(jnp.float32),
        offset_sums.reshape(heads, 16 * span),
        (((1,), (1,)), ((), ())),
        precision=HIGH,
        preferred_element_type=jnp.float32,
    )


def dot_nt(a, b):
    return lax.dot_general(a, b, (((1,), (1,)), ((), ())), preferred_element_type=jnp.float32)


def dot_tn(a, b):
    return lax.dot_general(a, b, (((0,), (0,)), ((), ())), preferred_element_type=jnp.float32)


def dot_nn(a, b):
    return lax.dot_general(a, b, (((1,), (0,)), ((), ())), preferred_element_type=jnp.float32)


def split_heads(block):
    lane = lax.broadcasted_iota(jnp.int32, block.shape, 1)
    zero = jnp.zeros_like(block)
    return jnp.where(lane < DK, block, zero), jnp.where(lane < DK, zero, block)


def attend_kernel(block, keys_count, causal, biased, *refs):
    if biased:
        qseg, kseg, base, q_ref, k_ref, v_ref, e_ref, c_ref, inv_ref, strip = refs
    else:
        qseg, kseg, q_ref, k_ref, v_ref, e_ref, c_ref, inv_ref = refs
    i = pl.program_id(1)
    if biased:
        wide = 2 * keys_count

        @pl.when(i == 0)
        def _():
            for head in range(2):
                rows = base[0, head]
                for a in range(block // 8):
                    strip[head, 8 * a : 8 * a + 8, :] = pltpu.roll(rows, (8 * a + wide - block) % wide, 1)

    allowed = qseg[...] == kseg[...]
    if causal:
        rows = lax.broadcasted_iota(jnp.int32, (block, keys_count), 0) + i * block
        allowed = allowed & (lax.broadcasted_iota(jnp.int32, (block, keys_count), 1) <= rows)
    q_heads = split_heads(q_ref[...])
    v_heads = split_heads(v_ref[...])
    inverses = []
    context = None
    for head in range(2):
        scores = dot_nt(q_heads[head], k_ref[...])
        if biased:
            start = pl.multiple_of((keys_count // block - 1 - i) * block, block)
            scores = scores + strip[head, :, pl.ds(start, keys_count)]
        scores = jnp.where(allowed, scores, NEG)
        highest = jnp.max(scores, axis=1, keepdims=True)
        weights = jnp.exp(scores - highest)
        inverses.append(1.0 / jnp.sum(weights, axis=1, keepdims=True))
        weights = weights.astype(jnp.bfloat16)
        e_ref[head] = weights
        part = dot_nn(weights, v_heads[head])
        context = part if context is None else context + part
    lane = lax.broadcasted_iota(jnp.int32, (block, PAIR), 1)
    inverse = jnp.where(lane < DK, inverses[0], inverses[1])
    inv_ref[...] = inverse
    c_ref[...] = (context * inverse).astype(jnp.bfloat16)


def attend_back_kernel(block, keys_count, steps, biased, *refs):
    if biased:
        q_ref, k_ref, v_ref, e_ref, c_ref, inv_ref, gc_ref, gq_ref, gk_ref, gv_ref, off_ref, gk_sum, gv_sum, strip = refs
    else:
        q_ref, k_ref, v_ref, e_ref, c_ref, inv_ref, gc_ref, gq_ref, gk_ref, gv_ref, gk_sum, gv_sum = refs
    i = pl.program_id(1)

    @pl.when(i == 0)
    def _():
        gk_sum[...] = jnp.zeros_like(gk_sum)
        gv_sum[...] = jnp.zeros_like(gv_sum)
        if biased:
            strip[...] = jnp.zeros_like(strip)

    scaled = (gc_ref[...].astype(jnp.float32) * inv_ref[...]).astype(jnp.bfloat16)
    product = scaled.astype(jnp.float32) * c_ref[...].astype(jnp.float32)
    lane = lax.broadcasted_iota(jnp.int32, (block, PAIR), 1)
    inner = (
        jnp.sum(jnp.where(lane < DK, product, 0.0), axis=1, keepdims=True),
        jnp.sum(jnp.where(lane < DK, 0.0, product), axis=1, keepdims=True),
    )
    g_heads = split_heads(scaled)
    q_heads = split_heads(q_ref[...])
    k_heads = split_heads(k_ref[...])
    gq = None
    for head in range(2):
        weights = e_ref[head]
        grad = dot_nt(g_heads[head], v_ref[...])
        grad = weights.astype(jnp.float32) * (grad - inner[head])
        if biased:
            start = pl.multiple_of((keys_count // block - 1 - i) * block, block)
            strip[head, :, pl.ds(start, keys_count)] += grad
        grad = grad.astype(jnp.bfloat16)
        part = dot_nn(grad, k_heads[head])
        gq = part if gq is None else gq + part
        gk_sum[...] += dot_tn(grad, q_heads[head])
        gv_sum[...] += dot_tn(weights, g_heads[head])
    gq_ref[...] = gq.astype(jnp.bfloat16)

    @pl.when(i == steps - 1)
    def _():
        gk_ref[...] = gk_sum[...].astype(jnp.bfloat16)
        gv_ref[...] = gv_sum[...].astype(jnp.bfloat16)
        if biased:
            wide = 2 * keys_count
            for head in range(2):
                total = jnp.zeros((8, wide), jnp.float32)
                for a in range(block // 8):
                    total = total + pltpu.roll(strip[head, 8 * a : 8 * a + 8, :], (block - 8 * a) % wide, 1)
                off_ref[0, head] = total


def attend_forward(query, keys, values, base, query_segments, key_segments, causal):
    count, cols = query.shape[0], keys.shape[0]
    pairs = query.shape[1] // PAIR
    block = min(256, count)
    steps = count // block
    row_spec = pl.BlockSpec((block, PAIR), lambda h, i: (i, h))
    key_spec = pl.BlockSpec((cols, PAIR), lambda h, i: (0, h))
    in_specs = [
        pl.BlockSpec((block, 1), lambda h, i: (i, 0)),
        pl.BlockSpec((1, cols), lambda h, i: (0, 0)),
    ]
    args = [query_segments[:, None], key_segments[None, :]]
    scratch = []
    if base is not None:
        in_specs.append(pl.BlockSpec((1, 2, 8, 2 * cols), lambda h, i: (h, 0, 0, 0)))
        args.append(base)
        scratch.append(pltpu.VMEM((2, block, 2 * cols), jnp.float32))
    return pl.pallas_call(
        functools.partial(attend_kernel, block, cols, causal, base is not None),
        grid=(pairs, steps),
        in_specs=in_specs + [row_spec, key_spec, key_spec],
        out_specs=[
            pl.BlockSpec((2, block, cols), lambda h, i: (h, i, 0)),
            row_spec,
            row_spec,
        ],
        out_shape=[
            jax.ShapeDtypeStruct((2 * pairs, count, cols), jnp.bfloat16),
            jax.ShapeDtypeStruct((count, pairs * PAIR), jnp.bfloat16),
            jax.ShapeDtypeStruct((count, pairs * PAIR), jnp.float32),
        ],
        scratch_shapes=scratch,
        compiler_params=pltpu.CompilerParams(vmem_limit_bytes=VMEM_BYTES),
        cost_estimate=pl.CostEstimate(
            flops=4 * count * cols * PAIR * 2 * pairs, bytes_accessed=2 * pairs * count * cols * 2, transcendentals=0
        ),
    )(*args, query, keys, values)


def attend_backward(query, keys, values, saved, grad_context, biased):
    weights, context, inverse = saved
    count, cols = query.shape[0], keys.shape[0]
    pairs = query.shape[1] // PAIR
    block = min(256, count)
    steps = count // block
    row_spec = pl.BlockSpec((block, PAIR), lambda h, i: (i, h))
    key_spec = pl.BlockSpec((cols, PAIR), lambda h, i: (0, h))
    out_specs = [row_spec, key_spec, key_spec]
    out_shape = [
        jax.ShapeDtypeStruct((count, pairs * PAIR), jnp.bfloat16),
        jax.ShapeDtypeStruct((cols, pairs * PAIR), jnp.bfloat16),
        jax.ShapeDtypeStruct((cols, pairs * PAIR), jnp.bfloat16),
    ]
    scratch = [pltpu.VMEM((cols, PAIR), jnp.float32), pltpu.VMEM((cols, PAIR), jnp.float32)]
    if biased:
        out_specs.append(pl.BlockSpec((1, 2, 8, 2 * cols), lambda h, i: (h, 0, 0, 0)))
        out_shape.append(jax.ShapeDtypeStruct((pairs, 2, 8, 2 * cols), jnp.float32))
        scratch.append(pltpu.VMEM((2, block, 2 * cols), jnp.float32))
    return pl.pallas_call(
        functools.partial(attend_back_kernel, block, cols, steps, biased),
        grid=(pairs, steps),
        in_specs=[
            row_spec,
            key_spec,
            key_spec,
            pl.BlockSpec((2, block, cols), lambda h, i: (h, i, 0)),
            row_spec,
            row_spec,
            row_spec,
        ],
        out_specs=out_specs,
        out_shape=out_shape,
        scratch_shapes=scratch,
        compiler_params=pltpu.CompilerParams(vmem_limit_bytes=VMEM_BYTES),
        cost_estimate=pl.CostEstimate(
            flops=8 * count * cols * PAIR * 2 * pairs, bytes_accessed=2 * pairs * count * cols * 2, transcendentals=0
        ),
    )(query, keys, values, weights, context, inverse, grad_context)


def ffn_backward(grad_rows, normed_rows, hidden, active, weight_up, weight_down):
    grad_active = jnp.einsum(
        "rd,fd->rf", grad_rows, weight_down, preferred_element_type=jnp.float32
    )
    grad_down = jnp.einsum("rf,rd->fd", active, grad_rows, preferred_element_type=jnp.float32)
    unused, pull = jax.vjp(gelu_tanh, hidden)
    grad_hidden = pull(grad_active)[0].astype(jnp.bfloat16)
    grad_up = jnp.einsum("rd,rf->df", normed_rows, grad_hidden, preferred_element_type=jnp.float32)
    grad_normed = jnp.einsum(
        "rf,df->rd", grad_hidden, weight_up, preferred_element_type=jnp.float32
    )
    return (grad_normed, grad_up, grad_down)


def norm_backward(values, gain, grad_normed):
    unused, pull = jax.vjp(rms_norm, values, gain)
    return pull(grad_normed)


def on_device(
    enc_input,
    dec_input,
    enc_lengths,
    dec_lengths,
    attn_query,
    attn_kv,
    attn_out,
    ffn_up,
    ffn_down,
    gains,
    rel_bias,
    enc_cotangent,
    dec_cotangent,
):
    weights = (
        lax.all_gather(attn_query, "wide", axis=1, tiled=True),
        lax.all_gather(attn_kv, "wide", axis=2, tiled=True),
        lax.all_gather(attn_out, "wide", axis=2, tiled=True),
        lax.all_gather(ffn_up, "wide", axis=1, tiled=True),
        lax.all_gather(ffn_down, "wide", axis=2, tiled=True),
    )
    gain_rows = gains.astype(jnp.float32)
    heads_local = rel_bias.shape[2]
    enc_segments = segment_ids(enc_lengths[0], ENC)
    dec_segments = segment_ids(dec_lengths[0], DEC)

    side = lax.axis_index("narrow")
    swap = [(0, 1), (1, 0)]

    def spread_rows(values):
        own = values.astype(jnp.bfloat16)
        other = lax.ppermute(own, "narrow", swap)
        return jnp.where(side == 0, jnp.concatenate([own, other]), jnp.concatenate([other, own]))

    def collect_rows(parts):
        half = parts.shape[0] // 2
        parts = parts.astype(jnp.bfloat16)
        other = lax.ppermute(lax.dynamic_slice_in_dim(parts, (1 - side) * half, half), "narrow", swap)
        own = lax.dynamic_slice_in_dim(parts, side * half, half)
        return own.astype(jnp.float32) + other.astype(jnp.float32)

    def attention_layer(normed_query, normed_keys, layer, base, query_segments, key_segments, causal):
        query = jnp.dot(normed_query, weights[0][layer], preferred_element_type=jnp.float32).astype(jnp.bfloat16)
        keys = jnp.dot(normed_keys, weights[1][layer, 0], preferred_element_type=jnp.float32).astype(jnp.bfloat16)
        values = jnp.dot(normed_keys, weights[1][layer, 1], preferred_element_type=jnp.float32).astype(jnp.bfloat16)
        saved = attend_forward(query, keys, values, base, query_segments, key_segments, causal)
        parts = jnp.dot(saved[1], weights[2][layer], preferred_element_type=jnp.float32)
        return ((query, keys, values, saved), collect_rows(parts))

    enc_start = enc_input.astype(jnp.float32)
    rows_a = spread_rows(rms_norm(enc_start, gain_rows[0]))
    kept_a, branch = attention_layer(
        rows_a, rows_a, 0, base_rows(rel_bias[0], ENC, True), enc_segments, enc_segments, False
    )
    enc_mid = enc_start + branch
    rows_b = spread_rows(rms_norm(enc_mid, gain_rows[1]))
    hidden_b = jnp.dot(rows_b, weights[3][0], preferred_element_type=jnp.float32)
    active_b = gelu_tanh(hidden_b).astype(jnp.bfloat16)
    enc_final = enc_mid + collect_rows(
        jnp.dot(active_b, weights[4][0], preferred_element_type=jnp.float32)
    )
    memory = spread_rows(rms_norm(enc_final, gain_rows[5]))
    dec_start = dec_input.astype(jnp.float32)
    rows_c = spread_rows(rms_norm(dec_start, gain_rows[2]))
    kept_c, branch = attention_layer(
        rows_c, rows_c, 1, base_rows(rel_bias[1], DEC, False), dec_segments, dec_segments, True
    )
    dec_one = dec_start + branch
    rows_d = spread_rows(rms_norm(dec_one, gain_rows[3]))
    kept_d, branch = attention_layer(
        rows_d, memory, 2, None, dec_segments, enc_segments, False
    )
    dec_two = dec_one + branch
    rows_e = spread_rows(rms_norm(dec_two, gain_rows[4]))
    hidden_e = jnp.dot(rows_e, weights[3][1], preferred_element_type=jnp.float32)
    active_e = gelu_tanh(hidden_e).astype(jnp.bfloat16)
    dec_final = dec_two + collect_rows(
        jnp.dot(active_e, weights[4][1], preferred_element_type=jnp.float32)
    )
    def attention_back(grad_state, kept, normed_query, normed_keys, layer, span, two_sided):
        grad_rows = spread_rows(grad_state)
        query, keys, values, saved = kept
        grad_context = dot_nt(grad_rows, weights[2][layer]).astype(jnp.bfloat16)
        grad_out = dot_tn(saved[1], grad_rows)
        result = attend_backward(query, keys, values, saved, grad_context, span > 0)
        grad_q, grad_k, grad_v = result[:3]
        sums = [
            dot_tn(normed_query, grad_q),
            dot_tn(normed_keys, grad_k),
            dot_tn(normed_keys, grad_v),
            grad_out,
            table_grad(result[3], span, two_sided) if span else None,
        ]
        query_part = dot_nt(grad_q, weights[0][layer])
        key_part = dot_nt(grad_k, weights[1][layer, 0]) + dot_nt(grad_v, weights[1][layer, 1])
        return (query_part, key_part, sums)

    grad_dec = dec_cotangent.astype(jnp.float32)
    grad_normed, up_e, down_e = ffn_backward(
        spread_rows(grad_dec), rows_e, hidden_e, active_e, weights[3][1], weights[4][1]
    )
    grad_back, gain_e = norm_backward(dec_two, gain_rows[4], collect_rows(grad_normed))
    grad_dec = grad_dec + grad_back
    query_part, memory_part, sums_d = attention_back(
        grad_dec, kept_d, rows_d, memory, 2, 0, False
    )
    grad_normed, grad_memory = collect_rows(query_part), collect_rows(memory_part)
    grad_back, gain_d = norm_backward(dec_one, gain_rows[3], grad_normed)
    grad_dec = grad_dec + grad_back
    query_part, key_part, sums_c = attention_back(
        grad_dec, kept_c, rows_c, rows_c, 1, DEC, False
    )
    grad_back, gain_c = norm_backward(dec_start, gain_rows[2], collect_rows(query_part + key_part))
    grad_dec = grad_dec + grad_back
    grad_enc = enc_cotangent.astype(jnp.float32)
    grad_back, gain_m = norm_backward(enc_final, gain_rows[5], grad_memory)
    grad_enc = grad_enc + grad_back
    grad_normed, up_b, down_b = ffn_backward(
        spread_rows(grad_enc), rows_b, hidden_b, active_b, weights[3][0], weights[4][0]
    )
    grad_back, gain_b = norm_backward(enc_mid, gain_rows[1], collect_rows(grad_normed))
    grad_enc = grad_enc + grad_back
    query_part, key_part, sums_a = attention_back(
        grad_enc, kept_a, rows_a, rows_a, 0, ENC, True
    )
    grad_back, gain_a = norm_backward(enc_start, gain_rows[0], collect_rows(query_part + key_part))
    grad_enc = grad_enc + grad_back
    grad_query = jnp.stack([sums_a[0], sums_c[0], sums_d[0]])
    grad_kv = jnp.stack(
        [
            jnp.stack([sums_a[1], sums_a[2]]),
            jnp.stack([sums_c[1], sums_c[2]]),
            jnp.stack([sums_d[1], sums_d[2]]),
        ]
    )
    grad_out = jnp.stack([sums_a[3], sums_c[3], sums_d[3]])
    grad_up = jnp.stack([up_b, up_e])
    grad_down = jnp.stack([down_b, down_e])
    tiles = (
        lax.psum_scatter(
            grad_query.astype(jnp.bfloat16), "wide", scatter_dimension=1, tiled=True
        ).astype(jnp.float32),
        lax.psum_scatter(
            grad_kv.astype(jnp.bfloat16), "wide", scatter_dimension=2, tiled=True
        ).astype(jnp.float32),
        lax.psum_scatter(
            grad_out.astype(jnp.bfloat16), "wide", scatter_dimension=2, tiled=True
        ).astype(jnp.float32),
        lax.psum_scatter(
            grad_up.astype(jnp.bfloat16), "wide", scatter_dimension=1, tiled=True
        ).astype(jnp.float32),
        lax.psum_scatter(
            grad_down.astype(jnp.bfloat16), "wide", scatter_dimension=2, tiled=True
        ).astype(jnp.float32),
    )
    tiles = (
        lax.psum(tiles[0].astype(jnp.bfloat16), "dp").astype(jnp.float32),
        lax.psum(tiles[1].astype(jnp.bfloat16), "dp").astype(jnp.float32),
        lax.psum(tiles[2].astype(jnp.bfloat16), "dp").astype(jnp.float32),
        lax.psum(tiles[3].astype(jnp.bfloat16), "dp").astype(jnp.float32),
        lax.psum(tiles[4].astype(jnp.bfloat16), "dp").astype(jnp.float32),
    )
    gain_grads = jnp.stack([gain_a, gain_b, gain_c, gain_d, gain_e, gain_m])
    column = lax.axis_index("narrow") * heads_local
    bias_local = jnp.stack([sums_a[4], sums_c[4]])
    bias_full = lax.dynamic_update_slice(
        jnp.zeros((2, NB, H), jnp.float32), bias_local, (0, 0, column)
    )
    gain_total, bias_total = lax.psum((gain_grads, bias_full), ("dp", "wide", "narrow"))
    bias_grad = lax.dynamic_slice(bias_total, (0, 0, column), (2, NB, heads_local))
    return (
        enc_final.astype(jnp.bfloat16),
        dec_final.astype(jnp.bfloat16),
        grad_enc,
        grad_dec,
        tiles[0],
        tiles[1],
        tiles[2],
        tiles[3],
        tiles[4],
        gain_total,
        bias_grad,
    )


def solution(mesh):
    return jax.shard_map(
        on_device,
        mesh=mesh,
        in_specs=(
            P(("dp", "wide", "narrow"), None),
            P(("dp", "wide", "narrow"), None),
            P(("dp", "wide"), None),
            P(("dp", "wide"), None),
            P(None, "wide", "narrow"),
            P(None, None, "wide", "narrow"),
            P(None, "narrow", "wide"),
            P(None, "wide", "narrow"),
            P(None, "narrow", "wide"),
            P(),
            P(None, None, "narrow"),
            P(("dp", "wide", "narrow"), None),
            P(("dp", "wide", "narrow"), None),
        ),
        out_specs=(
            P(("dp", "wide", "narrow"), None),
            P(("dp", "wide", "narrow"), None),
            P(("dp", "wide", "narrow"), None),
            P(("dp", "wide", "narrow"), None),
            P(None, "wide", "narrow"),
            P(None, None, "wide", "narrow"),
            P(None, "narrow", "wide"),
            P(None, "wide", "narrow"),
            P(None, "narrow", "wide"),
            P(),
            P(None, None, "narrow"),
        ),
        check_vma=False,
    )
```

profile of v0, /device:TPU:0, one launch (start us, length us, event | category | flops | bytes accessed | tf_op | source)
XLA Modules:
  0.0 1065.7 jit_solution(5629924697420951568)
XLA Ops:
  11.6 2.9 collective-permute-start
  17.6 14.5 %collective-permute-done = bf16[512,768]{1,0:T(8,128)(2,1)S(1)} collective-permute-done((bf16[512,768]{1,0:T(8,128)(2,1)S(1)}, bf16[512,768]{1,0:T(8,128)(2,1)S(1)}, u32[]{:S(2)}, u32[]{:S(2)}) %collective-permute-start) | collective-permute-done | bytes 786464 | tf_op jit(solution)/shard_map/ppermute | solution.py:339
  32.1 26.5 %all-gather.6.cloned.1.call-done = bf16[3,768,384]{2,1,0:T(8,128)(2,1)} async-done(((bf16[3,96,384]{2,1,0:T(8,128)(2,1)}), bf16[3,768,384]{2,1,0:T(8,128)(2,1)}) %all-gather.6.cloned.1.call-update) | async-done | bytes 1769488 | tf_op jit(solution)/shard_map/all_gather | solution.py:323
  58.6 2.9 convolution_convert_fusion.10.refs_3_.refs_0_
  61.5 63.5 %all-gather.8.cloned.1.call-done = bf16[3,2,768,384]{3,2,1,0:T(8,128)(2,1)} async-done(((bf16[3,2,96,384]{3,2,1,0:T(8,128)(2,1)}), bf16[3,2,768,384]{3,2,1,0:T(8,128)(2,1)}) %all-gather.8.cloned.1.call-update) | async-done | bytes 3538960 | tf_op jit(solution)/shard_map/all_gather | solution.py:324
  125.0 2.9 convolution_convert_fusion.8.refs_5_.refs_2_
  127.9 2.9 convolution_convert_fusion.9.refs_4_.refs_1_
  130.9 21.1 %shard_map.212 = (bf16[6,1024,1024]{2,1,0:T(8,128)(2,1)}, bf16[1024,384]{1,0:T(8,128)(2,1)}, f32[1024,384]{1,0:T(8,128)}) custom-call(s32[1024,1]{1,0:T(8,128)} %copy.45.refs_0_, s32[1,1024]{1,0:T(1,128)} %bitcast.201, f32[3,2,8,2048]{3,2,1,0:T(8,128)} %bitcast.194, bf16[1024,384]{1,0:T(8,128)(2,1)} %convolution_convert_fusion.10.refs_3_.refs_0_, ...), custom_call_target="tpu_custom_call" | custom-call | flops 3221225472 | bytes 12582912 | tf_op jit(solution)/shard_map/pallas_call | solution.py:225
  151.9 19.4 %all-gather.10.cloned.1.call-done = bf16[3,384,768]{1,2,0:T(8,128)(2,1)} async-done(((bf16[3,384,96]{1,2,0:T(8,128)(2,1)}), bf16[3,384,768]{1,2,0:T(8,128)(2,1)}) %all-gather.10.cloned.1.call-update) | async-done | bytes 1769488 | tf_op jit(solution)/shard_map/all_gather | solution.py:325
  178.5 16.8 %collective-permute-done.1 = bf16[512,768]{1,0:T(8,128)(2,1)S(1)} collective-permute-done((bf16[512,768]{1,0:T(8,128)(2,1)S(1)}, bf16[512,768]{1,0:T(8,128)(2,1)S(1)}, u32[]{:S(2)}, u32[]{:S(2)}) %collective-permute-start.1) | collective-permute-done | bytes 786464 | tf_op jit(solution)/shard_map/ppermute | solution.py:345
  207.2 4.7 shard_map.213
  214.4 37.9 %all-gather.12.cloned.1.call-done = bf16[2,768,1536]{2,1,0:T(8,128)(2,1)} async-done(((bf16[2,96,1536]{2,1,0:T(8,128)(2,1)}), bf16[2,768,1536]{2,1,0:T(8,128)(2,1)}) %all-gather.12.cloned.1.call-update) | async-done | bytes 4718608 | tf_op jit(solution)/shard_map/all_gather | solution.py:326
  252.3 7.3 fusion.14
  259.6 72.8 %all-gather.14.cloned.1.call-done = bf16[2,1536,768]{1,2,0:T(8,128)(2,1)} async-done(((bf16[2,1536,96]{1,2,0:T(8,128)(2,1)}), bf16[2,1536,768]{1,2,0:T(8,128)(2,1)}) %all-gather.14.cloned.1.call-update) | async-done | bytes 4718608 | tf_op jit(solution)/shard_map/all_gather | solution.py:327
  332.4 7.2 fusion.23
  343.8 18.5 %collective-permute-done.5 = bf16[128,768]{1,0:T(8,128)(2,1)S(1)} collective-permute-done((bf16[128,768]{1,0:T(8,128)(2,1)S(1)}, bf16[128,768]{1,0:T(8,128)(2,1)S(1)}, u32[]{:S(2)}, u32[]{:S(2)}) %collective-permute-start.5) | collective-permute-done | bytes 196640 | tf_op jit(solution)/shard_map/ppermute | solution.py:345
  366.8 19.5 %collective-permute-done.6 = bf16[128,768]{1,0:T(8,128)(2,1)S(1)} collective-permute-done((bf16[128,768]{1,0:T(8,128)(2,1)S(1)}, bf16[128,768]{1,0:T(8,128)(2,1)S(1)}, u32[]{:S(2)}, u32[]{:S(2)}) %collective-permute-start.6) | collective-permute-done | bytes 196640 | tf_op jit(solution)/shard_map/ppermute | solution.py:339
  392.2 6.1 shard_map.214
  401.5 5.3 collective-permute-done.8
  409.2 3.6 collective-permute-done.9
  416.7 3.1 fusion.33
  422.2 5.7 collective-permute-done.12
  430.4 4.2 collective-permute-done.13
  436.8 6.7 shard_map.215
  448.3 14.4 %collective-permute-done.14 = bf16[512,768]{1,0:T(8,128)(2,1)S(1)} collective-permute-done((bf16[512,768]{1,0:T(8,128)(2,1)S(1)}, bf16[512,768]{1,0:T(8,128)(2,1)S(1)}, u32[]{:S(2)}, u32[]{:S(2)}) %collective-permute-start.14) | collective-permute-done | bytes 786464 | tf_op jit(solution)/shard_map/ppermute | solution.py:345
  469.6 7.0 collective-permute-done.15
  477.5 4.1 fusion.8
  481.6 2.6 pad_maximum_fusion.1
  484.2 12.7 %copy.49 = bf16[2,1536,768]{1,0,2:T(2,128)(2,1)} copy(bf16[2,1536,768]{2,1,0:T(8,128)(2,1)} %pad_maximum_fusion.1) | data formatting | bytes 9437184 | tf_op jit(solution)/shard_map/stack | solution.py:445
  496.9 9.8 fusion.6
  506.8 5.4 fusion.24
  514.8 2.8 fusion.55
  518.8 14.4 %collective-permute-done.19 = bf16[128,768]{1,0:T(8,128)(2,1)S(1)} collective-permute-done((bf16[128,768]{1,0:T(8,128)(2,1)S(1)}, bf16[128,768]{1,0:T(8,128)(2,1)S(1)}, u32[]{:S(2)}, u32[]{:S(2)}) %collective-permute-start.19) | collective-permute-done | bytes 196640 | tf_op jit(solution)/shard_map/ppermute | solution.py:345
  542.0 10.5 collective-permute-done.20
  555.3 4.0 copy.53
  563.7 4.5 shard_map.217
  571.8 25.4 %shard_map.216 = (bf16[1024,384]{1,0:T(8,128)(2,1)}, bf16[1024,384]{1,0:T(8,128)(2,1)}, bf16[1024,384]{1,0:T(8,128)(2,1)}, f32[3,2,8,2048]{3,2,1,0:T(8,128)}) custom-call(bf16[1024,384]{1,0:T(8,128)(2,1)} %convolution_convert_fusion.10.refs_3_.refs_0_, bf16[1024,384]{1,0:T(8,128)(2,1)} %convolution_convert_fusion.9.refs_4_.refs_1_, ...), custom_call_target="tpu_custom_call" | custom-call | flops 6442450944 | bytes 12582912 | tf_op jit(solution)/shard_map/pallas_call | solution.py:266
  617.5 5.0 fusion.7
  638.7 3.7 fusion.61
  642.4 24.4 %all-reduce.6.cloned.1.call-done = bf16[2,1536,768]{1,0,2:T(2,128)(2,1)} async-done(((bf16[2,1536,768]{1,0,2:T(2,128)(2,1)}), bf16[2,1536,768]{1,0,2:T(2,128)(2,1)}) %all-reduce.6.cloned.1.call-update) | async-done | bytes 4718608
  669.1 66.3 %reduce-scatter.13.cloned.1.call-done = bf16[96,1152]{1,0:T(8,128)(2,1)} async-done(((bf16[768,1152]{1,0:T(8,128)(2,1)}), bf16[96,1152]{1,0:T(8,128)(2,1)}) %reduce-scatter.13.cloned.1.call-update) | async-done | bytes 221200
  739.0 65.1 %reduce-scatter.7.cloned.1.call-done = bf16[3,96,384]{2,1,0:T(8,128)(2,1)} async-done(((bf16[3,768,384]{2,1,0:T(8,128)(2,1)}), bf16[3,96,384]{2,1,0:T(8,128)(2,1)}) %reduce-scatter.7.cloned.1.call-update) | async-done | bytes 221200 | tf_op jit(solution)/shard_map/reduce_scatter | solution.py:447
  804.1 81.7 %reduce-scatter.9.cloned.1.call-done = bf16[3,2,96,384]{3,2,1,0:T(8,128)(2,1)} async-done(((bf16[3,2,768,384]{3,2,1,0:T(8,128)(2,1)}), bf16[3,2,96,384]{3,2,1,0:T(8,128)(2,1)}) %reduce-scatter.9.cloned.1.call-update) | async-done | bytes 442384 | tf_op jit(solution)/shard_map/reduce_scatter | solution.py:450
  885.8 98.3 %reduce-scatter.11.cloned.1.call-done = bf16[2,96,1536]{2,1,0:T(8,128)(2,1)} async-done(((bf16[2,768,1536]{2,1,0:T(8,128)(2,1)}), bf16[2,96,1536]{2,1,0:T(8,128)(2,1)}) %reduce-scatter.11.cloned.1.call-update) | async-done | bytes 589840 | tf_op jit(solution)/shard_map/reduce_scatter | solution.py:456
  984.2 3.3 add_convert_fusion
  992.3 14.8 %collective-permute-done.18 = bf16[512,768]{1,0:T(8,128)(2,1)S(1)} collective-permute-done((bf16[512,768]{1,0:T(8,128)(2,1)S(1)}, bf16[512,768]{1,0:T(8,128)(2,1)S(1)}, u32[]{:S(2)}, u32[]{:S(2)}) %collective-permute-start.18) | collective-permute-done | bytes 786464 | tf_op jit(solution)/shard_map/ppermute | solution.py:345
  1007.9 41.2 %all-reduce.1 = (f32[6,768]{1,0:T(8,128)}, f32[2,32,12]{1,0,2:T(2,128)S(1)}) all-reduce(f32[6,768]{1,0:T(8,128)S(1)} %stack.153, f32[2,32,12]{1,0,2:T(2,128)S(1)} %copy_dynamic-update-slice_fusion), channel_id=1, replica_groups=mesh['dp'=2,'wide'=8,'narrow'=2] {'dp','wide','narrow'}, use_global_device_ids=true, to_apply=%region_32.33 | all-reduce | flops 5376 | bytes 43008 | tf_op jit(solution)/shard_map/psum | solution.py:476
  1049.8 2.8 fusion.36
  (475 shorter events, 148.6 us)
Async XLA Ops:
  7.2 51.4 %all-gather.6.cloned.1.call-start = ((), (), s32[]{:S(2)}) async-start(), calls=%async_computation.4 | async-start | bytes 1990656 | tf_op jit(solution)/shard_map/all_gather | solution.py:323
  7.9 117.1 %all-gather.8.cloned.1.call-start = ((), (), s32[]{:S(2)}) async-start(), calls=%async_computation.5 | async-start | bytes 3981312 | tf_op jit(solution)/shard_map/all_gather | solution.py:324
  8.7 162.7 %all-gather.10.cloned.1.call-start = ((), (), s32[]{:S(2)}) async-start(), calls=%async_computation.6 | async-start | bytes 1990656 | tf_op jit(solution)/shard_map/all_gather | solution.py:325
  9.4 242.9 %all-gather.12.cloned.1.call-start = ((), (), s32[]{:S(2)}) async-start(), calls=%async_computation.7 | async-start | bytes 5308416 | tf_op jit(solution)/shard_map/all_gather | solution.py:326
  10.0 322.4 %all-gather.14.cloned.1.call-start = ((), (), s32[]{:S(2)}) async-start(), calls=%async_computation.8 | async-start | bytes 5308416 | tf_op jit(solution)/shard_map/all_gather | solution.py:327
  10.6 656.3 %all-reduce.6.cloned.1.call-start = ((), (), s32[]{:S(2)}) async-start(), calls=%async_computation.13 | async-start | bytes 9437184
  10.7 165.7 %copy-start.71 = (f32[768]{0:T(1024)}, f32[768]{0:T(1024)S(1)}, u32[]{:S(2)}) copy-start(f32[768]{0:T(1024)S(1)} %get-tuple-element.110) | copy-start | bytes 9220
  11.6 116.3 %copy-start.35 = (bf16[512,768]{1,0:T(8,128)(2,1)}, bf16[512,768]{1,0:T(8,128)(2,1)S(1)}, u32[]{:S(2)}) copy-start(bf16[512,768]{1,0:T(8,128)(2,1)S(1)} %fusion.25) | copy-start | bytes 2359300
  11.6 20.5 %collective-permute-start = (bf16[512,768]{1,0:T(8,128)(2,1)S(1)}, bf16[512,768]{1,0:T(8,128)(2,1)S(1)}, u32[]{:S(2)}, u32[]{:S(2)}) collective-permute-start(bf16[512,768]{1,0:T(8,128)(2,1)S(1)} %fusion.25), channel_id=1, source_target_pairs={{0,1},{1,0},{2,3},{3,2},{4,5},{5,4},{6,7},{7,6},{8,9},{9,8},{10,11... | collective-permute-start | bytes 2359304 | tf_op jit(solution)/shard_map/ppermute | solution.py:339
  14.7 46.9 %copy-start.53 = (s32[16384]{0:T(1024)}, s32[16384]{0:T(1024)S(1)}, u32[]{:S(2)}) copy-start(s32[16384]{0:T(1024)S(1)} %fusion.81) | copy-start | bytes 196612
  16.4 45.2 %copy-start.93 = (s32[1024]{0:T(1024)}, s32[1024]{0:T(1024)S(1)}, u32[]{:S(2)}) copy-start(s32[1024]{0:T(1024)S(1)} %convert_reduce_fusion) | copy-start | bytes 12292
  17.5 44.0 %copy-start.110 = (f32[128]{0:T(128)}, f32[128]{0:T(128)S(1)}, u32[]{:S(2)}) copy-start(f32[128]{0:T(128)S(1)} %fusion.72) | copy-start | bytes 1540
  17.5 158.9 %copy-start.101 = (f32[128]{0:T(128)}, f32[128]{0:T(128)S(1)}, u32[]{:S(2)}) copy-start(f32[128]{0:T(128)S(1)} %fusion.89) | copy-start | bytes 1540
  32.1 95.9 %copy-start.115 = (bf16[512,768]{1,0:T(8,128)(2,1)}, bf16[512,768]{1,0:T(8,128)(2,1)S(1)}, u32[]{:S(2)}) copy-start(bf16[512,768]{1,0:T(8,128)(2,1)S(1)} %collective-permute-done) | copy-start | bytes 2359300
  174.9 20.4 %collective-permute-start.1 = (bf16[512,768]{1,0:T(8,128)(2,1)S(1)}, bf16[512,768]{1,0:T(8,128)(2,1)S(1)}, u32[]{:S(2)}, u32[]{:S(2)}) collective-permute-start(bf16[512,768]{1,0:T(8,128)(2,1)S(1)} %constant_dynamic-slice_fusion.11), channel_id=1, source_target_pairs={{0,1},{1,0},{2,3},{3,2},{4,5},{5,4},{6,7},{7,6},{8,9},{9,8},{10,11... | collective-permute-start | bytes 2359304 | tf_op jit(solution)/shard_map/ppermute | solution.py:345
  176.5 28.3 %copy-start.63 = (bf16[128,768]{1,0:T(8,128)(2,1)}, bf16[128,768]{1,0:T(8,128)(2,1)S(1)}, u32[]{:S(2)}) copy-start(bf16[128,768]{1,0:T(8,128)(2,1)S(1)} %fusion.67) | copy-start | bytes 589828
  176.5 23.7 %collective-permute-start.4 = (bf16[128,768]{1,0:T(8,128)(2,1)S(1)}, bf16[128,768]{1,0:T(8,128)(2,1)}, u32[]{:S(2)}, u32[]{:S(2)}) collective-permute-start(bf16[128,768]{1,0:T(8,128)(2,1)S(1)} %fusion.67), channel_id=1, source_target_pairs={{0,1},{1,0},{2,3},{3,2},{4,5},{5,4},{6,7},{7,6},{8,9},{9,8},{10,11... | collective-permute-start | bytes 589832 | tf_op jit(solution)/shard_map/ppermute | solution.py:339
  197.1 55.2 %copy-start.38 = (bf16[512,768]{1,0:T(8,128)(2,1)}, bf16[512,768]{1,0:T(8,128)(2,1)S(1)}, u32[]{:S(2)}) copy-start(bf16[512,768]{1,0:T(8,128)(2,1)S(1)} %multiply_convert_fusion.3) | copy-start | bytes 2359300
  197.1 17.2 %collective-permute-start.2 = (bf16[512,768]{1,0:T(8,128)(2,1)S(1)}, bf16[512,768]{1,0:T(8,128)(2,1)}, u32[]{:S(2)}, u32[]{:S(2)}) collective-permute-start(bf16[512,768]{1,0:T(8,128)(2,1)S(1)} %multiply_convert_fusion.3), channel_id=1, source_target_pairs={{0,1},{1,0},{2,3},{3,2},{4,5},{5,4},{6,7},{7,6},{8,9},{9,8},{10,11... | collective-permute-start | bytes 2359304 | tf_op jit(solution)/shard_map/ppermute | solution.py:339
  339.7 22.8 %collective-permute-start.3 = (bf16[512,768]{1,0:T(8,128)(2,1)S(1)}, bf16[512,768]{1,0:T(8,128)(2,1)}, u32[]{:S(2)}, u32[]{:S(2)}) collective-permute-start(bf16[512,768]{1,0:T(8,128)(2,1)S(1)} %constant_dynamic-slice_fusion.10), channel_id=1, source_target_pairs={{0,1},{1,0},{2,3},{3,2},{4,5},{5,4},{6,7},{7,6},{8,9},{9,8},{10,11... | collective-permute-start | bytes 2359304 | tf_op jit(solution)/shard_map/ppermute | solution.py:345
  342.8 19.5 %collective-permute-start.5 = (bf16[128,768]{1,0:T(8,128)(2,1)S(1)}, bf16[128,768]{1,0:T(8,128)(2,1)S(1)}, u32[]{:S(2)}, u32[]{:S(2)}) collective-permute-start(bf16[128,768]{1,0:T(8,128)(2,1)S(1)} %constant_dynamic-slice_fusion.9), channel_id=1, source_target_pairs={{0,1},{1,0},{2,3},{3,2},{4,5},{5,4},{6,7},{7,6},{8,9},{9,8},{10,11... | collective-permute-start | bytes 589832 | tf_op jit(solution)/shard_map/ppermute | solution.py:345
  364.3 99.6 %copy-start.77 = (f32[512]{0:T(512)}, f32[512]{0:T(512)S(1)}, u32[]{:S(2)}) copy-start(f32[512]{0:T(512)S(1)} %fusion.88) | copy-start | bytes 6148
  364.5 25.9 %copy-start.40 = (bf16[512,768]{1,0:T(8,128)(2,1)}, bf16[512,768]{1,0:T(8,128)(2,1)S(1)}, u32[]{:S(2)}) copy-start(bf16[512,768]{1,0:T(8,128)(2,1)S(1)} %multiply_convert_fusion.2) | copy-start | bytes 2359300
  364.5 23.9 %collective-permute-start.7 = (bf16[512,768]{1,0:T(8,128)(2,1)S(1)}, bf16[512,768]{1,0:T(8,128)(2,1)S(1)}, u32[]{:S(2)}, u32[]{:S(2)}) collective-permute-start(bf16[512,768]{1,0:T(8,128)(2,1)S(1)} %multiply_convert_fusion.2), channel_id=1, source_target_pairs={{0,1},{1,0},{2,3},{3,2},{4,5},{5,4},{6,7},{7,6},{8,9},{9,8},{10,11... | collective-permute-start | bytes 2359304 | tf_op jit(solution)/shard_map/ppermute | solution.py:339
  366.2 20.1 %collective-permute-start.6 = (bf16[128,768]{1,0:T(8,128)(2,1)S(1)}, bf16[128,768]{1,0:T(8,128)(2,1)S(1)}, u32[]{:S(2)}, u32[]{:S(2)}) collective-permute-start(bf16[128,768]{1,0:T(8,128)(2,1)S(1)} %multiply_convert_fusion.5), channel_id=1, source_target_pairs={{0,1},{1,0},{2,3},{3,2},{4,5},{5,4},{6,7},{7,6},{8,9},{9,8},{10,11... | collective-permute-start | bytes 589832 | tf_op jit(solution)/shard_map/ppermute | solution.py:339
  399.9 6.8 collective-permute-start.8
  407.1 5.7 collective-permute-start.9
  408.6 6.9 collective-permute-start.11
  420.7 7.2 collective-permute-start.12
  428.9 5.7 collective-permute-start.13
  446.8 15.9 %collective-permute-start.14 = (bf16[512,768]{1,0:T(8,128)(2,1)S(1)}, bf16[512,768]{1,0:T(8,128)(2,1)S(1)}, u32[]{:S(2)}, u32[]{:S(2)}) collective-permute-start(bf16[512,768]{1,0:T(8,128)(2,1)S(1)} %constant_dynamic-slice_fusion.5), channel_id=1, source_target_pairs={{0,1},{1,0},{2,3},{3,2},{4,5},{5,4},{6,7},{7,6},{8,9},{9,8},{10,11... | collective-permute-start | bytes 2359304 | tf_op jit(solution)/shard_map/ppermute | solution.py:345
  464.5 12.1 %collective-permute-start.15 = (bf16[512,768]{1,0:T(8,128)(2,1)S(1)}, bf16[512,768]{1,0:T(8,128)(2,1)S(1)}, u32[]{:S(2)}, u32[]{:S(2)}) collective-permute-start(bf16[512,768]{1,0:T(8,128)(2,1)S(1)} %fusion.109), channel_id=1, source_target_pairs={{0,1},{1,0},{2,3},{3,2},{4,5},{5,4},{6,7},{7,6},{8,9},{9,8},{10,11... | collective-permute-start | bytes 2359304 | tf_op jit(solution)/shard_map/ppermute | solution.py:339
  496.9 238.5 %reduce-scatter.13.cloned.1.call-start = ((), (), s32[]{:S(2)}) async-start(), calls=%async_computation.12 | async-start | bytes 1990656
  512.3 21.7 %collective-permute-start.16 = (bf16[512,768]{1,0:T(8,128)(2,1)S(1)}, bf16[512,768]{1,0:T(8,128)(2,1)S(1)}, u32[]{:S(2)}, u32[]{:S(2)}) collective-permute-start(bf16[512,768]{1,0:T(8,128)(2,1)S(1)} %constant_dynamic-slice_fusion.4), channel_id=1, source_target_pairs={{0,1},{1,0},{2,3},{3,2},{4,5},{5,4},{6,7},{7,6},{8,9},{9,8},{10,11... | collective-permute-start | bytes 2359304 | tf_op jit(solution)/shard_map/ppermute | solution.py:345
  513.8 19.4 %collective-permute-start.19 = (bf16[128,768]{1,0:T(8,128)(2,1)S(1)}, bf16[128,768]{1,0:T(8,128)(2,1)S(1)}, u32[]{:S(2)}, u32[]{:S(2)}) collective-permute-start(bf16[128,768]{1,0:T(8,128)(2,1)S(1)} %constant_dynamic-slice_fusion.2), channel_id=1, source_target_pairs={{0,1},{1,0},{2,3},{3,2},{4,5},{5,4},{6,7},{7,6},{8,9},{9,8},{10,11... | collective-permute-start | bytes 589832 | tf_op jit(solution)/shard_map/ppermute | solution.py:345
  517.6 22.3 %collective-permute-start.10 = (bf16[128,768]{1,0:T(8,128)(2,1)S(1)}, bf16[128,768]{1,0:T(8,128)(2,1)S(1)}, u32[]{:S(2)}, u32[]{:S(2)}) collective-permute-start(bf16[128,768]{1,0:T(8,128)(2,1)S(1)} %constant_dynamic-slice_fusion.7), channel_id=1, source_target_pairs={{0,1},{1,0},{2,3},{3,2},{4,5},{5,4},{6,7},{7,6},{8,9},{9,8},{10,11... | collective-permute-start | bytes 589832 | tf_op jit(solution)/shard_map/ppermute | solution.py:345
  538.3 14.6 %collective-permute-start.17 = (bf16[512,768]{1,0:T(8,128)(2,1)S(1)}, bf16[512,768]{1,0:T(8,128)(2,1)S(1)}, u32[]{:S(2)}, u32[]{:S(2)}) collective-permute-start(bf16[512,768]{1,0:T(8,128)(2,1)S(1)} %get-tuple-element.122), channel_id=1, source_target_pairs={{0,1},{1,0},{2,3},{3,2},{4,5},{5,4},{6,7},{7,6},{8,9},{9,8},{10,11... | collective-permute-start | bytes 2359304 | tf_op jit(solution)/shard_map/ppermute | solution.py:339
  541.0 11.5 %collective-permute-start.20 = (bf16[128,768]{1,0:T(8,128)(2,1)S(1)}, bf16[128,768]{1,0:T(8,128)(2,1)S(1)}, u32[]{:S(2)}, u32[]{:S(2)}) collective-permute-start(bf16[128,768]{1,0:T(8,128)(2,1)S(1)} %get-tuple-element.120), channel_id=1, source_target_pairs={{0,1},{1,0},{2,3},{3,2},{4,5},{5,4},{6,7},{7,6},{8,9},{9,8},{10,11... | collective-permute-start | bytes 589832 | tf_op jit(solution)/shard_map/ppermute | solution.py:339
  560.9 243.3 %reduce-scatter.7.cloned.1.call-start = ((), (), s32[]{:S(2)}) async-start(), calls=%async_computation.9 | async-start | bytes 1990656 | tf_op jit(solution)/shard_map/reduce_scatter | solution.py:447
  571.8 25.4 %copy-start.36 = (bf16[512,768]{1,0:T(8,128)(2,1)S(1)}, bf16[512,768]{1,0:T(8,128)(2,1)}, u32[]{:S(2)}) copy-start(bf16[512,768]{1,0:T(8,128)(2,1)} %copy-done.35) | copy-start | bytes 2359300
  571.8 25.4 %copy-start.116 = (bf16[512,768]{1,0:T(8,128)(2,1)S(1)}, bf16[512,768]{1,0:T(8,128)(2,1)}, u32[]{:S(2)}) copy-start(bf16[512,768]{1,0:T(8,128)(2,1)} %copy-done.115) | copy-start | bytes 2359300
  600.9 285.0 %reduce-scatter.9.cloned.1.call-start = ((), (), s32[]{:S(2)}) async-start(), calls=%async_computation.10 | async-start | bytes 3981312 | tf_op jit(solution)/shard_map/reduce_scatter | solution.py:450
  615.5 368.7 %reduce-scatter.11.cloned.1.call-start = ((), (), s32[]{:S(2)}) async-start(), calls=%async_computation.11 | async-start | bytes 5308416 | tf_op jit(solution)/shard_map/reduce_scatter | solution.py:456
  625.2 427.4 %all-reduce.8.cloned.1.call-start = ((), (), s32[]{:S(2)}) async-start(), calls=%async_computation.14 | async-start | bytes 4276224 | tf_op jit(solution)/shard_map/psum | solution.py:466
  629.9 5.7 collective-permute-start.21
  987.7 19.3 %collective-permute-start.18 = (bf16[512,768]{1,0:T(8,128)(2,1)S(1)}, bf16[512,768]{1,0:T(8,128)(2,1)S(1)}, u32[]{:S(2)}, u32[]{:S(2)}) collective-permute-start(bf16[512,768]{1,0:T(8,128)(2,1)S(1)} %constant_dynamic-slice_fusion.3), channel_id=1, source_target_pairs={{0,1},{1,0},{2,3},{3,2},{4,5},{5,4},{6,7},{7,6},{8,9},{9,8},{10,11... | collective-permute-start | bytes 2359304 | tf_op jit(solution)/shard_map/ppermute | solution.py:345
  991.1 58.6 %copy-start.86 = (f32[512]{0:T(512)S(1)}, f32[512]{0:T(512)}, u32[]{:S(2)}) copy-start(f32[512]{0:T(512)} %copy-done.85) | copy-start | bytes 6148
  991.1 58.6 %copy-start.9 = (f32[512,768]{1,0:T(8,128)S(1)}, f32[512,768]{1,0:T(8,128)}, u32[]{:S(2)}) copy-start(f32[512,768]{1,0:T(8,128)} %get-tuple-element.123) | copy-start | bytes 4718596
  (129 other events, 750.5 us)
Sparse Core Ops, SparseCore 0:
  10.2 48.3 all-gather.5
  60.8 64.1 all-gather.7
  127.2 44.0 all-gather.9
  173.4 78.8 all-gather.11
  254.3 78.0 all-gather.13
  497.0 169.7 all-reduce.5
  670.3 65.0 reduce-scatter.12
  739.3 64.8 reduce-scatter.6
  807.8 78.0 reduce-scatter.8
  889.3 94.7 reduce-scatter.10
  987.4 21.3 all-reduce.7
where the time goes:
time: 1080 us; the launch traced here: 1070 us
  waiting for transfers between devices  712 us (66%)
  matrix products  119 us (11%)
  Pallas kernels  68.3 us (6%)
  local copies, waits for them, and re-layouts  44.5 us (4%)
  blocking collectives  41.2 us (4%)
  other arithmetic  34.1 us (3%)
  starting transfers between devices  30.4 us (3%)
  between operations  16.8 us (2%)
    reduce_scatter x1, waiting for transfers between devices, on_device(): lax.psum_scatter(grad_up.astype(jnp.bfloat16), 'wide', scatter_dimension=...  98.3 us
    unnamed x13, waiting for transfers between devices  93.9 us
    ppermute x11, waiting for transfers between devices, collect_rows(): lax.ppermute(lax.dynamic_slice_in_dim(parts, (1 - side) * half, half), 'n...  90.7 us
    reduce_scatter x1, waiting for transfers between devices, on_device(): lax.psum_scatter(grad_kv.astype(jnp.bfloat16), 'wide', scatter_dimension=...  81.7 us
    all_gather x1, waiting for transfers between devices, on_device(): lax.all_gather(ffn_down, 'wide', axis=2, tiled=True)  72.8 us
    reduce_scatter x1, waiting for transfers between devices, on_device(): lax.psum_scatter(grad_query.astype(jnp.bfloat16), 'wide', scatter_dimensi...  65.1 us
    all_gather x1, waiting for transfers between devices, on_device(): lax.all_gather(attn_kv, 'wide', axis=2, tiled=True)  63.5 us
    ppermute x11, waiting for transfers between devices, spread_rows(): other = lax.ppermute(own, 'narrow', swap)  61.9 us
  transfers between devices with their start and end apart: 33, of which 25 were waited for; matrix products, arithmetic and copies ran while one was open for 13% of the time, Pallas kernels for 5%

commit v1 on v0

--- a/solution.py
+++ b/solution.py
@@ -19,7 +19,9 @@
 EPS = 1e-06
 NEG = -1e30
 HIGH = lax.Precision.HIGHEST
-VMEM_BYTES = 56 * 2**20
+VMEM_BYTES = 60 * 2**20
+GELU_A = math.sqrt(2.0 / math.pi)
+GELU_B = 0.044715
 
 
 def cutoffs(exact, buckets):
@@ -285,6 +287,462 @@
     )(query, keys, values, weights, context, inverse, grad_context)
 
 
+MESH_IDS = pl.DeviceIdType.MESH
+CHUNK = 256
+ATT = 4 * 384
+
+
+def any_spec():
+    return pl.BlockSpec(memory_space=pl.ANY)
+
+
+def vmem_spec():
+    return pl.BlockSpec(memory_space=pltpu.VMEM)
+
+
+def normed(values, gain):
+    return values * lax.rsqrt(jnp.mean(values * values, axis=1, keepdims=True) + EPS) * gain
+
+
+def gelu_pair(values):
+    square = values * values
+    inner = jnp.tanh(GELU_A * values * (1.0 + GELU_B * square))
+    half = 0.5 * (1.0 + inner)
+    slope = half + 0.5 * values * (1.0 - inner * inner) * (GELU_A * (1.0 + 3.0 * GELU_B * square))
+    return values * half, slope
+
+
+class Place:
+    def __init__(self, wide):
+        self.core = lax.axis_index("dp")
+        self.wide = lax.axis_index("wide")
+        self.side = lax.axis_index("narrow")
+        self.count = wide
+        self.fars = wide // 2
+        self.far = self.wide // 2
+        self.near = self.wide % 2
+
+    def sibling(self):
+        return (1 - self.core, self.wide, self.side)
+
+    def across(self):
+        return (self.core, self.wide, 1 - self.side)
+
+    def beside(self):
+        return (self.core, 2 * self.far + 1 - self.near, self.side)
+
+    def along(self, step):
+        return (self.core, 2 * lax.rem(self.far + step, self.fars) + self.near, self.side)
+
+    def index_from(self, step):
+        return 2 * lax.rem(self.far - step + self.fars, self.fars) + self.near
+
+    def index_beside(self, step):
+        return 2 * lax.rem(self.far - step + self.fars, self.fars) + 1 - self.near
+
+    def greet(self):
+        partners = [self.sibling(), self.across(), self.beside()]
+        partners += [self.along(step) for step in range(1, self.fars)]
+        barrier = pltpu.get_barrier_semaphore()
+        for partner in partners:
+            pl.semaphore_signal(barrier, inc=1, device_id=partner, device_id_type=MESH_IDS)
+        pl.semaphore_wait(barrier, len(partners))
+
+
+def remote(source, target, send, receive, partner):
+    return pltpu.make_async_remote_copy(
+        src_ref=source,
+        dst_ref=target,
+        send_sem=send,
+        recv_sem=receive,
+        device_id=partner,
+        device_id_type=MESH_IDS,
+    )
+
+
+class Gather:
+    def __init__(self, place, pack, groups, send, receive, local):
+        self.place, self.pack, self.groups = place, pack, groups
+        self.send, self.receive, self.local = send, receive, local
+        self.rows = pack.shape[0]
+        self.sent = []
+
+    def at(self, group, index, core):
+        first, width, target, offset = self.groups[group]
+        half = width // 2
+        start = pl.multiple_of(offset + core * half, 128)
+        return target.at[pl.ds(pl.multiple_of(index * self.rows, 16), self.rows), pl.ds(start, half)]
+
+    def own(self, group):
+        first, width, target, offset = self.groups[group]
+        half = width // 2
+        return self.pack.at[:, pl.ds(pl.multiple_of(first + self.place.core * half, 128), half)]
+
+    def local_copy(self, group):
+        first, width, target, offset = self.groups[group]
+        rows = pl.ds(pl.multiple_of(self.place.wide * self.rows, 16), self.rows)
+        return pltpu.make_async_copy(
+            self.pack.at[:, pl.ds(first, width)], target.at[rows, pl.ds(offset, width)], self.local.at[group]
+        )
+
+    def push(self, group, slot, source, index, partner):
+        copy = remote(
+            source,
+            self.at(group, index, self.place.core),
+            self.send.at[group, slot],
+            self.receive.at[group, slot],
+            partner,
+        )
+        copy.start()
+        self.sent.append(copy)
+
+    def await_slot(self, group, slot, index, core):
+        block = self.at(group, index, core)
+        remote(block, block, self.send.at[group, slot], self.receive.at[group, slot], self.place.sibling()).wait_recv()
+
+    def start(self, group):
+        place, fars = self.place, self.place.fars
+        for step in range(1, fars):
+            self.push(group, step - 1, self.own(group), place.wide, place.along(step))
+        self.push(group, fars - 1, self.own(group), place.wide, place.beside())
+        self.local_copy(group).start()
+
+    def relay_along(self, group):
+        place, fars = self.place, self.place.fars
+        for step in range(1, fars):
+            index = place.index_from(step)
+            self.await_slot(group, step - 1, index, place.core)
+            block = self.at(group, index, place.core)
+            self.push(group, fars - 1 + step, block, index, place.beside())
+            self.push(group, 2 * fars - 2 + step, block, index, place.sibling())
+
+    def relay_beside(self, group):
+        place, fars = self.place, self.place.fars
+        for step in range(fars):
+            index = place.index_beside(step)
+            self.await_slot(group, fars - 1 + step, index, place.core)
+            block = self.at(group, index, place.core)
+            self.push(group, 3 * fars - 2 + step, block, index, place.sibling())
+
+    def finish(self, group):
+        place, fars = self.place, self.place.fars
+        for step in range(1, fars):
+            self.await_slot(group, 2 * fars - 2 + step, place.index_from(step), 1 - place.core)
+        for step in range(fars):
+            self.await_slot(group, 3 * fars - 2 + step, place.index_beside(step), 1 - place.core)
+        self.local_copy(group).wait()
+
+    def close(self):
+        for copy in self.sent:
+            copy.wait_send()
+
+
+def gather_slots(wide):
+    return 4 * (wide // 2) - 2
+
+
+def softmax_pair(q_pair, k_pair, v_pair, allowed, biases, e_store):
+    q_heads = split_heads(q_pair)
+    v_heads = split_heads(v_pair)
+    inverses = []
+    context = None
+    for head in range(2):
+        scores = dot_nt(q_heads[head], k_pair)
+        if biases is not None:
+            scores = scores + biases(head)
+        scores = jnp.where(allowed, scores, NEG)
+        highest = jnp.max(scores, axis=1, keepdims=True)
+        weights = jnp.exp(scores - highest)
+        inverses.append(1.0 / jnp.sum(weights, axis=1, keepdims=True))
+        weights = weights.astype(jnp.bfloat16)
+        e_store(head, weights)
+        part = dot_nn(weights, v_heads[head])
+        context = part if context is None else context + part
+    lane = lax.broadcasted_iota(jnp.int32, context.shape, 1)
+    inverse = jnp.where(lane < DK, inverses[0], inverses[1])
+    return inverse, (context * inverse).astype(jnp.bfloat16)
+
+
+def build_strip(strip, base, pairs, block, span):
+    def one(pair, carry):
+        for head in range(2):
+            rows = base[pair, head]
+            for a in range(block // 8):
+                strip[2 * pair + head, 8 * a : 8 * a + 8, :] = pltpu.roll(rows, (8 * a + 2 * span - block) % (2 * span), 1)
+        return carry
+
+    lax.fori_loop(0, pairs, one, 0)
+
+
+def enc_forward_kernel(
+    wide,
+    x_own,
+    pack,
+    gains,
+    base,
+    qseg,
+    kseg,
+    w1,
+    w2,
+    n0,
+    qkv,
+    c,
+    inv,
+    e_all,
+    e1,
+    n1,
+    slope_all,
+    a_all,
+    ef,
+    mem,
+    x_full,
+    strip,
+    e_buf,
+    slope_buf,
+    a_buf,
+    y_send,
+    y_recv,
+    g_send,
+    g_recv,
+    g_local,
+    x_sems,
+    y_sems,
+    z_sems,
+    l_sems,
+):
+    place = Place(wide)
+    side = place.side
+    half = x_own.shape[0]
+    rows = 2 * half
+    steps = rows // CHUNK
+    width = c.shape[1]
+    ffn = a_all.shape[1]
+    pairs = width // PAIR
+    place.greet()
+    gather = Gather(
+        place,
+        pack,
+        [
+            (0, 4 * width, w1, 0),
+            (4 * width, 2 * ffn, w1, 4 * width),
+            (4 * width + 2 * ffn, 8 * width, w2, 0),
+            (12 * width + 2 * ffn, 2 * ffn, w2, 8 * width),
+        ],
+        g_send,
+        g_recv,
+        g_local,
+    )
+    mine = pl.ds(pl.multiple_of(side * half, 16), half)
+    swap_x = remote(x_own, x_full.at[mine], x_sems.at[0], x_sems.at[1], place.across())
+    gather.start(0)
+    swap_x.start()
+    keep_x = pltpu.make_async_copy(x_own, x_full.at[mine], l_sems.at[6])
+    keep_x.start()
+    build_strip(strip, base, pairs, CHUNK, rows)
+    gather.relay_along(0)
+    gather.start(1)
+    keep_x.wait()
+    gather.relay_beside(0)
+    swap_x.wait()
+
+    def norm_rows(i, carry):
+        at = pl.ds(pl.multiple_of(i * CHUNK, CHUNK), CHUNK)
+        n0[at, :] = normed(x_full[at, :].astype(jnp.float32), gains[0:1, :]).astype(jnp.bfloat16)
+        return carry
+
+    lax.fori_loop(0, steps, norm_rows, 0)
+    gather.finish(0)
+
+    def project(i, carry):
+        at = pl.ds(pl.multiple_of(i * CHUNK, CHUNK), CHUNK)
+        qkv[at, :] = dot_nn(n0[at, :], w1[:, : 3 * width]).astype(jnp.bfloat16)
+        return carry
+
+    lax.fori_loop(0, steps, project, 0)
+
+    def lanes(base_lane, pair):
+        return pl.ds(pl.multiple_of(base_lane + pair * PAIR, PAIR), PAIR)
+
+    def save(i, kind):
+        slot = i % 2
+        at = pl.ds(i * CHUNK, CHUNK)
+        if kind == 0:
+            return pltpu.make_async_copy(e_buf.at[slot], e_all.at[:, at, :], l_sems.at[slot])
+        if kind == 1:
+            return pltpu.make_async_copy(slope_buf.at[slot], slope_all.at[at, :], l_sems.at[2 + slot])
+        return pltpu.make_async_copy(a_buf.at[slot], a_all.at[at, :], l_sems.at[4 + slot])
+
+    def swap_y(layer, i):
+        at = pl.ds(i * CHUNK, CHUNK)
+        sems = y_sems if layer == 0 else z_sems
+        return remote(y_send.at[layer, at], y_recv.at[layer, at], sems.at[0, i], sems.at[1, i], place.across())
+
+    def attend(i):
+        at = slice(i * CHUNK, (i + 1) * CHUNK)
+        slot = i % 2
+        if i >= 2:
+            save(i - 2, 0).wait()
+        first = (steps - 1 - i) * CHUNK
+
+        def one(pair, carry):
+            allowed = qseg[at, :] == kseg[...]
+
+            def bias(head):
+                return strip[2 * pair + head, :, first : first + rows]
+
+            def store(head, weights):
+                e_buf[slot, 2 * pair + head] = weights
+
+            inverse, context = softmax_pair(
+                qkv[at, lanes(0, pair)],
+                qkv[:, lanes(width, pair)],
+                qkv[:, lanes(2 * width, pair)],
+                allowed,
+                bias,
+                store,
+            )
+            inv[at, lanes(0, pair)] = inverse
+            c[at, lanes(0, pair)] = context
+            return carry
+
+        lax.fori_loop(0, pairs, one, 0)
+        save(i, 0).start()
+        y_send[0, at, :] = dot_nt(c[at, :], w1[:, 3 * width : 4 * width]).astype(jnp.bfloat16)
+        swap_y(0, i).start()
+
+    def feed(i):
+        at = slice(i * CHUNK, (i + 1) * CHUNK)
+        slot = i % 2
+        swap_y(0, i).wait_recv()
+        both = y_send[0, at, :].astype(jnp.float32) + y_recv[0, at, :].astype(jnp.float32)
+        middle = x_full[at, :].astype(jnp.float32) + both
+        e1[at, :] = middle
+        rounded = normed(middle, gains[1:2, :]).astype(jnp.bfloat16)
+        n1[at, :] = rounded
+        if i >= 2:
+            save(i - 2, 1).wait()
+            save(i - 2, 2).wait()
+
+        def part(j, carry):
+            cols = pl.ds(pl.multiple_of(4 * width + j * width, PAIR), width)
+            here = pl.ds(pl.multiple_of(j * width, PAIR), width)
+            active, slope = gelu_pair(dot_nn(n1[at, :], w1[:, cols]))
+            a_buf[slot, :, here] = active.astype(jnp.bfloat16)
+            slope_buf[slot, :, here] = slope.astype(jnp.bfloat16)
+            return carry
+
+        lax.fori_loop(0, ffn // width, part, 0)
+        save(i, 1).start()
+        save(i, 2).start()
+        y_send[1, at, :] = dot_nt(a_buf[slot], w1[:, 4 * width + ffn :]).astype(jnp.bfloat16)
+        swap_y(1, i).start()
+
+    def last(i):
+        at = slice(i * CHUNK, (i + 1) * CHUNK)
+        swap_y(1, i).wait_recv()
+        both = y_send[1, at, :].astype(jnp.float32) + y_recv[1, at, :].astype(jnp.float32)
+        final = e1[at, :] + both
+        ef[at, :] = final
+        mem[at, :] = normed(final, gains[5:6, :]).astype(jnp.bfloat16)
+
+    attend(0)
+    gather.relay_along(1)
+    gather.start(2)
+    attend(1)
+    gather.relay_beside(1)
+    attend(2)
+    gather.finish(1)
+    feed(0)
+    gather.relay_along(2)
+    gather.start(3)
+    attend(3)
+    feed(1)
+    gather.relay_beside(2)
+    feed(2)
+    gather.relay_along(3)
+    feed(3)
+    last(0)
+    last(1)
+    gather.relay_beside(3)
+    last(2)
+    last(3)
+    gather.finish(2)
+    gather.finish(3)
+    gather.close()
+    for i in range(steps):
+        swap_y(0, i).wait_send()
+        swap_y(1, i).wait_send()
+    for i in range(steps - 2, steps):
+        for kind in range(3):
+            save(i, kind).wait()
+
+
+def enc_forward(wide, x_own, pack, gains, base, segments):
+    half, model = x_own.shape
+    rows = 2 * half
+    pairs = base.shape[0]
+    width = pairs * PAIR
+    ffn = (pack.shape[1] - 12 * width) // 4
+    bf, f32 = jnp.bfloat16, jnp.float32
+    shape = jax.ShapeDtypeStruct
+    slots = gather_slots(wide)
+    steps = rows // CHUNK
+    return pl.pallas_call(
+        functools.partial(enc_forward_kernel, wide),
+        in_specs=[vmem_spec(), any_spec(), vmem_spec(), vmem_spec(), vmem_spec(), vmem_spec()],
+        out_shape=[
+            shape((model, 4 * width + 2 * ffn), bf),
+            shape((model, 8 * width + 2 * ffn), bf),
+            shape((rows, model), bf),
+            shape((rows, 3 * width), bf),
+            shape((rows, width), bf),
+            shape((rows, width), f32),
+            shape((2 * pairs, rows, rows), bf),
+            shape((rows, model), f32),
+            shape((rows, model), bf),
+            shape((rows, ffn), bf),
+            shape((rows, ffn), bf),
+            shape((rows, model), f32),
+            shape((rows, model), bf),
+        ],
+        out_specs=[
+            vmem_spec(),
+            any_spec(),
+            vmem_spec(),
+            vmem_spec(),
+            vmem_spec(),
+            vmem_spec(),
+            any_spec(),
+            vmem_spec(),
+            vmem_spec(),
+            any_spec(),
+            any_spec(),
+            vmem_spec(),
+            vmem_spec(),
+        ],
+        scratch_shapes=[
+            pltpu.VMEM((rows, model), bf),
+            pltpu.VMEM((2 * pairs, CHUNK, 2 * rows), f32),
+            pltpu.VMEM((2, 2 * pairs, CHUNK, rows), bf),
+            pltpu.VMEM((2, CHUNK, ffn), bf),
+            pltpu.VMEM((2, CHUNK, ffn), bf),
+            pltpu.VMEM((2, rows, model), bf),
+            pltpu.VMEM((2, rows, model), bf),
+            pltpu.SemaphoreType.DMA((4, slots)),
+            pltpu.SemaphoreType.DMA((4, slots)),
+            pltpu.SemaphoreType.DMA((4,)),
+            pltpu.SemaphoreType.DMA((2,)),
+            pltpu.SemaphoreType.DMA((2, steps)),
+            pltpu.SemaphoreType.DMA((2, steps)),
+            pltpu.SemaphoreType.DMA((7,)),
+        ],
+        compiler_params=pltpu.CompilerParams(
+            collective_id=0, has_side_effects=True, vmem_limit_bytes=VMEM_BYTES
+        ),
+        cost_estimate=pl.CostEstimate(flops=10**10, bytes_accessed=6 * 10**7, transcendentals=0),
+    )(x_own, pack, gains, base, segments[:, None], segments[None, :])
+
+
 def ffn_backward(grad_rows, normed_rows, hidden, active, weight_up, weight_down):
     grad_active = jnp.einsum(
         "rd,fd->rf", grad_rows, weight_down, preferred_element_type=jnp.float32
@@ -304,7 +762,218 @@
     return pull(grad_normed)
 
 
+def pack_shards(attn_query, attn_kv, attn_out, ffn_up, ffn_down):
+    def attention(layer):
+        return [attn_query[layer], attn_kv[layer, 0], attn_kv[layer, 1], attn_out[layer].T]
+
+    def feed(layer):
+        return [ffn_up[layer], ffn_down[layer].T]
+
+    return jnp.concatenate(attention(0) + feed(0) + attention(1) + attention(2) + feed(1), axis=1)
+
+
+def ffn_back(grad_rows, normed_rows, slope, active, weight_up, weight_down):
+    grad_active = dot_nn(grad_rows, weight_down)
+    grad_down = dot_tn(active, grad_rows)
+    grad_hidden = (slope.astype(jnp.float32) * grad_active).astype(jnp.bfloat16)
+    return dot_nt(grad_hidden, weight_up), dot_tn(normed_rows, grad_hidden), grad_down
+
+
 def on_device(
+    wide,
+    enc_input,
+    dec_input,
+    enc_lengths,
+    dec_lengths,
+    attn_query,
+    attn_kv,
+    attn_out,
+    ffn_up,
+    ffn_down,
+    gains,
+    rel_bias,
+    enc_cotangent,
+    dec_cotangent,
+):
+    gain_rows = gains.astype(jnp.float32)
+    heads_local = rel_bias.shape[2]
+    enc_segments = segment_ids(enc_lengths[0], ENC)
+    dec_segments = segment_ids(dec_lengths[0], DEC)
+
+    side = lax.axis_index("narrow")
+    swap = [(0, 1), (1, 0)]
+
+    def spread_rows(values):
+        own = values.astype(jnp.bfloat16)
+        other = lax.ppermute(own, "narrow", swap)
+        return jnp.where(side == 0, jnp.concatenate([own, other]), jnp.concatenate([other, own]))
+
+    def collect_rows(parts):
+        half = parts.shape[0] // 2
+        parts = parts.astype(jnp.bfloat16)
+        other = lax.ppermute(lax.dynamic_slice_in_dim(parts, (1 - side) * half, half), "narrow", swap)
+        own = lax.dynamic_slice_in_dim(parts, side * half, half)
+        return own.astype(jnp.float32) + other.astype(jnp.float32)
+
+    def attention_layer(normed_query, normed_keys, layer, base, query_segments, key_segments, causal):
+        query = jnp.dot(normed_query, weights_q[layer], preferred_element_type=jnp.float32).astype(jnp.bfloat16)
+        keys = jnp.dot(normed_keys, weights_k[layer], preferred_element_type=jnp.float32).astype(jnp.bfloat16)
+        values = jnp.dot(normed_keys, weights_v[layer], preferred_element_type=jnp.float32).astype(jnp.bfloat16)
+        saved = attend_forward(query, keys, values, base, query_segments, key_segments, causal)
+        parts = dot_nt(saved[1], weights_o[layer])
+        return ((query, keys, values, saved), collect_rows(parts))
+
+    pack = pack_shards(attn_query, attn_kv, attn_out, ffn_up, ffn_down)
+    w1, w2, rows_a, qkv_a, context_a, inverse_a, e_a, e1_full, rows_b, slope_b, active_b, ef_full, memory = enc_forward(
+        wide, enc_input, pack, gain_rows, base_rows(rel_bias[0], ENC, True), enc_segments
+    )
+    width = DK * heads_local
+    ffn = ffn_up.shape[2]
+    layer_columns = [w1[:, : 4 * width], w2[:, : 4 * width], w2[:, 4 * width : 8 * width]]
+    weights_q = [columns[:, :width] for columns in layer_columns]
+    weights_k = [columns[:, width : 2 * width] for columns in layer_columns]
+    weights_v = [columns[:, 2 * width : 3 * width] for columns in layer_columns]
+    weights_o = [columns[:, 3 * width :] for columns in layer_columns]
+    up = [w1[:, 4 * width : 4 * width + ffn], w2[:, 8 * width : 8 * width + ffn]]
+    down = [w1[:, 4 * width + ffn :], w2[:, 8 * width + ffn :]]
+    kept_a = (
+        qkv_a[:, :width],
+        qkv_a[:, width : 2 * width],
+        qkv_a[:, 2 * width :],
+        (e_a, context_a, inverse_a),
+    )
+    half = enc_input.shape[0]
+
+    def own_rows(full):
+        return lax.dynamic_slice_in_dim(full, side * half, half)
+
+    enc_start = enc_input.astype(jnp.float32)
+    enc_mid = own_rows(e1_full)
+    enc_final = own_rows(ef_full)
+    dec_start = dec_input.astype(jnp.float32)
+    rows_c = spread_rows(rms_norm(dec_start, gain_rows[2]))
+    kept_c, branch = attention_layer(
+        rows_c, rows_c, 1, base_rows(rel_bias[1], DEC, False), dec_segments, dec_segments, True
+    )
+    dec_one = dec_start + branch
+    rows_d = spread_rows(rms_norm(dec_one, gain_rows[3]))
+    kept_d, branch = attention_layer(
+        rows_d, memory, 2, None, dec_segments, enc_segments, False
+    )
+    dec_two = dec_one + branch
+    rows_e = spread_rows(rms_norm(dec_two, gain_rows[4]))
+    active_e, slope_e = gelu_pair(dot_nn(rows_e, up[1]))
+    active_e = active_e.astype(jnp.bfloat16)
+    dec_final = dec_two + collect_rows(
+        dot_nt(active_e, down[1])
+    )
+    def attention_back(grad_state, kept, normed_query, normed_keys, layer, span, two_sided):
+        grad_rows = spread_rows(grad_state)
+        query, keys, values, saved = kept
+        grad_context = dot_nn(grad_rows, weights_o[layer]).astype(jnp.bfloat16)
+        grad_out = dot_tn(saved[1], grad_rows)
+        result = attend_backward(query, keys, values, saved, grad_context, span > 0)
+        grad_q, grad_k, grad_v = result[:3]
+        sums = [
+            dot_tn(normed_query, grad_q),
+            dot_tn(normed_keys, grad_k),
+            dot_tn(normed_keys, grad_v),
+            grad_out,
+            table_grad(result[3], span, two_sided) if span else None,
+        ]
+        query_part = dot_nt(grad_q, weights_q[layer])
+        key_part = dot_nt(grad_k, weights_k[layer]) + dot_nt(grad_v, weights_v[layer])
+        return (query_part, key_part, sums)
+
+    grad_dec = dec_cotangent.astype(jnp.float32)
+    grad_normed, up_e, down_e = ffn_back(
+        spread_rows(grad_dec), rows_e, slope_e, active_e, up[1], down[1]
+    )
+    grad_back, gain_e = norm_backward(dec_two, gain_rows[4], collect_rows(grad_normed))
+    grad_dec = grad_dec + grad_back
+    query_part, memory_part, sums_d = attention_back(
+        grad_dec, kept_d, rows_d, memory, 2, 0, False
+    )
+    grad_normed, grad_memory = collect_rows(query_part), collect_rows(memory_part)
+    grad_back, gain_d = norm_backward(dec_one, gain_rows[3], grad_normed)
+    grad_dec = grad_dec + grad_back
+    query_part, key_part, sums_c = attention_back(
+        grad_dec, kept_c, rows_c, rows_c, 1, DEC, False
+    )
+    grad_back, gain_c = norm_backward(dec_start, gain_rows[2], collect_rows(query_part + key_part))
+    grad_dec = grad_dec + grad_back
+    grad_enc = enc_cotangent.astype(jnp.float32)
+    grad_back, gain_m = norm_backward(enc_final, gain_rows[5], grad_memory)
+    grad_enc = grad_enc + grad_back
+    grad_normed, up_b, down_b = ffn_back(
+        spread_rows(grad_enc), rows_b, slope_b, active_b, up[0], down[0]
+    )
+    grad_back, gain_b = norm_backward(enc_mid, gain_rows[1], collect_rows(grad_normed))
+    grad_enc = grad_enc + grad_back
+    query_part, key_part, sums_a = attention_back(
+        grad_enc, kept_a, rows_a, rows_a, 0, ENC, True
+    )
+    grad_back, gain_a = norm_backward(enc_start, gain_rows[0], collect_rows(query_part + key_part))
+    grad_enc = grad_enc + grad_back
+    grad_query = jnp.stack([sums_a[0], sums_c[0], sums_d[0]])
+    grad_kv = jnp.stack(
+        [
+            jnp.stack([sums_a[1], sums_a[2]]),
+            jnp.stack([sums_c[1], sums_c[2]]),
+            jnp.stack([sums_d[1], sums_d[2]]),
+        ]
+    )
+    grad_out = jnp.stack([sums_a[3], sums_c[3], sums_d[3]])
+    grad_up = jnp.stack([up_b, up_e])
+    grad_down = jnp.stack([down_b, down_e])
+    tiles = (
+        lax.psum_scatter(
+            grad_query.astype(jnp.bfloat16), "wide", scatter_dimension=1, tiled=True
+        ).astype(jnp.float32),
+        lax.psum_scatter(
+            grad_kv.astype(jnp.bfloat16), "wide", scatter_dimension=2, tiled=True
+        ).astype(jnp.float32),
+        lax.psum_scatter(
+            grad_out.astype(jnp.bfloat16), "wide", scatter_dimension=2, tiled=True
+        ).astype(jnp.float32),
+        lax.psum_scatter(
+            grad_up.astype(jnp.bfloat16), "wide", scatter_dimension=1, tiled=True
+        ).astype(jnp.float32),
+        lax.psum_scatter(
+            grad_down.astype(jnp.bfloat16), "wide", scatter_dimension=2, tiled=True
+        ).astype(jnp.float32),
+    )
+    tiles = (
+        lax.psum(tiles[0].astype(jnp.bfloat16), "dp").astype(jnp.float32),
+        lax.psum(tiles[1].astype(jnp.bfloat16), "dp").astype(jnp.float32),
+        lax.psum(tiles[2].astype(jnp.bfloat16), "dp").astype(jnp.float32),
+        lax.psum(tiles[3].astype(jnp.bfloat16), "dp").astype(jnp.float32),
+        lax.psum(tiles[4].astype(jnp.bfloat16), "dp").astype(jnp.float32),
+    )
+    gain_grads = jnp.stack([gain_a, gain_b, gain_c, gain_d, gain_e, gain_m])
+    column = lax.axis_index("narrow") * heads_local
+    bias_local = jnp.stack([sums_a[4], sums_c[4]])
+    bias_full = lax.dynamic_update_slice(
+        jnp.zeros((2, NB, H), jnp.float32), bias_local, (0, 0, column)
+    )
+    gain_total, bias_total = lax.psum((gain_grads, bias_full), ("dp", "wide", "narrow"))
+    bias_grad = lax.dynamic_slice(bias_total, (0, 0, column), (2, NB, heads_local))
+    return (
+        enc_final.astype(jnp.bfloat16),
+        dec_final.astype(jnp.bfloat16),
+        grad_enc,
+        grad_dec,
+        tiles[0],
+        tiles[1],
+        tiles[2],
+        tiles[3],
+        tiles[4],
+        gain_total,
+        bias_grad,
+    )
+
+
+def on_device_general(
     enc_input,
     dec_input,
     enc_lengths,
@@ -491,8 +1160,15 @@
 
 
 def solution(mesh):
+    wide = mesh.shape["wide"]
+
+    def body(*args):
+        if args[4].shape[1] % 16 or wide % 2:
+            return on_device_general(*args)
+        return on_device(wide, *args)
+
     return jax.shard_map(
-        on_device,
+        body,
         mesh=mesh,
         in_specs=(
             P(("dp", "wide", "narrow"), None),

time: 1080 us -> 868 us (0.80)
  waiting for transfers between devices: 712 us -> 431 us
  Pallas kernels: 68.3 us -> 167 us
  matrix products: 119 us -> 92.4 us
    all_gather x5 -> x0, waiting for transfers between devices: 220 us -> none  [the longest x1 72.8 us: on_device(): lax.all_gather(ffn_down, 'wide', axis=2, tiled=True)]
    pallas_call x0 -> x1, Pallas kernels: none -> 120 us  [enc_forward(): pl.pallas_call(functools.partial(enc_forward_kernel, wide), in_specs=[vme...]
    dot_general x24 -> x12, matrix products: 77.2 us -> 33.5 us  [the longest x6 19 us: dot_nn(): lax.dot_general(a, b, (((1,), (0,)), ((), ())), preferred_element_type=jn...]
    ppermute x11 -> x9, waiting for transfers between devices: 90.7 us -> 55.8 us  [collect_rows(): lax.ppermute(lax.dynamic_slice_in_dim(parts, (1 - side) * half, half), 'n...]
    ppermute x11 -> x8, waiting for transfers between devices: 61.9 us -> 30.4 us  [spread_rows(): other = lax.ppermute(own, 'narrow', swap)]
    pallas_call x3 -> x2, Pallas kernels: 31.8 us -> 10.6 us  [attend_forward(): pl.pallas_call(functools.partial(attend_kernel, block, cols, causal, base...]
    dot_general x12 -> x14, matrix products: 24.4 us -> 34.3 us  [dot_nt(): lax.dot_general(a, b, (((1,), (1,)), ((), ())), preferred_element_type=jn...]
    dot_general x12 -> x16, matrix products: 14.3 us -> 21.9 us  [dot_tn(): lax.dot_general(a, b, (((0,), (0,)), ((), ())), preferred_element_type=jn...]
  transfers between devices with their start and end apart: 33 -> 23, of which waited for: 25 -> 17; matrix products, arithmetic and copies ran while one was open for 13% -> 13% of each run, Pallas kernels for 5% -> 17%
where the time goes in v1:
time: 868 us; the launch traced here: 857 us
  waiting for transfers between devices  431 us (50%)
  Pallas kernels  167 us (19%)
  matrix products  92.4 us (11%)
  local copies, waits for them, and re-layouts  49.8 us (6%)
  blocking collectives  41.3 us (5%)
  other arithmetic  38.2 us (4%)
  starting transfers between devices  19.9 us (2%)
  between operations  16.8 us (2%)
    pallas_call x1, Pallas kernels, enc_forward(): pl.pallas_call(functools.partial(enc_forward_kernel, wide), in_specs=[vme...  120 us
    reduce_scatter x1, waiting for transfers between devices, on_device(): lax.psum_scatter(grad_up.astype(jnp.bfloat16), 'wide', scatter_dimension=...  98.3 us
    unnamed x8, waiting for transfers between devices  98.3 us
    reduce_scatter x1, waiting for transfers between devices, on_device(): lax.psum_scatter(grad_kv.astype(jnp.bfloat16), 'wide', scatter_dimension=...  81.5 us
    reduce_scatter x1, waiting for transfers between devices, on_device(): lax.psum_scatter(grad_query.astype(jnp.bfloat16), 'wide', scatter_dimensi...  66.8 us
    ppermute x9, waiting for transfers between devices, collect_rows(): lax.ppermute(lax.dynamic_slice_in_dim(parts, (1 - side) * half, half), 'n...  55.8 us
    psum x1, blocking collectives, on_device(): lax.psum((gain_grads, bias_full), ('dp', 'wide', 'narrow'))  41.3 us
    pallas_call x3, Pallas kernels, attend_backward(): pl.pallas_call(functools.partial(attend_back_kernel, block, cols, steps,...  36.3 us
  transfers between devices with their start and end apart: 23, of which 17 were waited for; matrix products, arithmetic and copies ran while one was open for 13% of the time, Pallas kernels for 17%

profile of v1, /device:TPU:0, one launch (start us, length us, event | category | flops | bytes accessed | tf_op | source)
XLA Modules:
  0.0 856.8 jit_solution(1219724443004993025)
XLA Ops:
  10.9 3.0 collective-permute-start
  19.3 120.3 %shard_map.212 = (bf16[768,4608]{1,0:T(8,128)(2,1)}, bf16[768,6144]{1,0:T(8,128)(2,1)}, bf16[1024,768]{1,0:T(8,128)(2,1)}, bf16[1024,1152]{1,0:T(8,128)(2,1)}, b...) custom-call(bf16[512,768]{1,0:T(8,128)(2,1)} %x_own.1, ...), custom_call_target="tpu_custom_call" | custom-call | flops 10000000000 | bytes 60000000 | tf_op jit(solution)/shard_map/pallas_call | solution.py:690
  148.1 4.6 shard_map.213
  155.8 3.0 convolution_convert_fusion.5.refs_4_.refs_2_
  162.2 2.9 convolution_convert_fusion.6.refs_3_.refs_1_
  169.1 6.1 shard_map.214
  177.8 5.2 collective-permute-done.3
  185.4 3.6 collective-permute-done.4
  189.0 2.5 fusion.15
  191.6 3.5 fusion.4
  195.2 2.8 fusion.43
  199.6 6.2 collective-permute-done.7
  207.7 4.7 collective-permute-done.8
  214.6 6.7 shard_map.215
  221.3 2.4 fusion.63
  229.4 10.6 %collective-permute-done.9 = bf16[512,768]{1,0:T(8,128)(2,1)} collective-permute-done((bf16[512,768]{1,0:T(8,128)(2,1)}, bf16[512,768]{1,0:T(8,128)(2,1)}, u32[]{:S(2)}, u32[]{:S(2)}) %collective-permute-start.9) | collective-permute-done | bytes 786464 | tf_op jit(solution)/shard_map/ppermute | solution.py:814
  240.0 3.0 multiply_reduce_fusion
  243.0 3.1 fusion.123
  248.5 9.6 %collective-permute-done.10 = bf16[512,768]{1,0:T(8,128)(2,1)S(1)} collective-permute-done((bf16[512,768]{1,0:T(8,128)(2,1)S(1)}, bf16[512,768]{1,0:T(8,128)(2,1)S(1)}, u32[]{:S(2)}, u32[]{:S(2)}) %collective-permute-start.10) | collective-permute-done | bytes 786464 | tf_op jit(solution)/shard_map/ppermute | solution.py:808
  259.0 3.0 fusion.1
  262.0 2.5 pad_maximum_fusion.1
  264.5 12.7 %copy.49 = bf16[2,1536,768]{1,0,2:T(2,128)(2,1)} copy(bf16[2,1536,768]{2,1,0:T(8,128)(2,1)} %pad_maximum_fusion.1) | data formatting | bytes 9437184 | tf_op jit(solution)/shard_map/stack | solution.py:928
  279.6 5.7 multiply_convert_fusion
  285.3 5.4 fusion.17
  293.0 3.5 fusion.46
  296.6 16.4 %collective-permute-done.14 = bf16[128,768]{1,0:T(8,128)(2,1)S(1)} collective-permute-done((bf16[128,768]{1,0:T(8,128)(2,1)S(1)}, bf16[128,768]{1,0:T(8,128)(2,1)S(1)}, u32[]{:S(2)}, u32[]{:S(2)}) %collective-permute-start.14) | collective-permute-done | bytes 196640 | tf_op jit(solution)/shard_map/ppermute | solution.py:814
  320.6 10.7 %collective-permute-done.15 = bf16[128,768]{1,0:T(8,128)(2,1)S(1)} collective-permute-done((bf16[128,768]{1,0:T(8,128)(2,1)S(1)}, bf16[128,768]{1,0:T(8,128)(2,1)S(1)}, u32[]{:S(2)}, u32[]{:S(2)}) %collective-permute-start.15) | collective-permute-done | bytes 196640 | tf_op jit(solution)/shard_map/ppermute | solution.py:808
  334.0 4.0 copy.53
  339.8 3.2 fusion.125
  346.1 4.3 shard_map.217
  351.9 2.9 convolution_convert_fusion.4.refs_6_
  354.9 25.2 %shard_map.216 = (bf16[1024,384]{1,0:T(8,128)(2,1)}, bf16[1024,384]{1,0:T(8,128)(2,1)}, bf16[1024,384]{1,0:T(8,128)(2,1)}, f32[3,2,8,2048]{3,2,1,0:T(8,128)}) custom-call(bf16[1024,384]{1,0:T(8,128)(2,1)} %get-tuple-element.152.refs_0_, bf16[1024,384]{1,0:T(8,128)(2,1)} %get-tuple-element.151.refs_1_, bf16[1024,384]{1,0:T(8,128)(2,1)} %get-tuple-element.150.refs_2_, ...), custom_call_target="tpu_custom_call" | custom-call | flops 6442450944 | bytes 12582912 | tf_op jit(solution)/shard_map/pallas_call | solution.py:268
  380.1 2.7 fusion.31
  385.4 2.5 fusion.38
  399.8 4.3 fusion
  404.1 2.6 pad_maximum_fusion
  414.0 2.4 dynamic-slice_convert_fusion
  422.1 3.7 fusion.55
  425.8 31.9 %all-reduce.6.cloned.1.call-done = bf16[2,1536,768]{1,0,2:T(2,128)(2,1)} async-done(((bf16[2,1536,768]{1,0,2:T(2,128)(2,1)}), bf16[2,1536,768]{1,0,2:T(2,128)(2,1)}) %all-reduce.6.cloned.1.call-update) | async-done | bytes 4718608
  460.1 66.3 %reduce-scatter.13.cloned.1.call-done = bf16[96,1152]{1,0:T(8,128)(2,1)} async-done(((bf16[768,1152]{1,0:T(8,128)(2,1)}), bf16[96,1152]{1,0:T(8,128)(2,1)}) %reduce-scatter.13.cloned.1.call-update) | async-done | bytes 221200
  528.3 66.8 %reduce-scatter.7.cloned.1.call-done = bf16[3,96,384]{2,1,0:T(8,128)(2,1)} async-done(((bf16[3,768,384]{2,1,0:T(8,128)(2,1)}), bf16[3,96,384]{2,1,0:T(8,128)(2,1)}) %reduce-scatter.7.cloned.1.call-update) | async-done | bytes 221200 | tf_op jit(solution)/shard_map/reduce_scatter | solution.py:930
  595.1 81.5 %reduce-scatter.9.cloned.1.call-done = bf16[3,2,96,384]{3,2,1,0:T(8,128)(2,1)} async-done(((bf16[3,2,768,384]{3,2,1,0:T(8,128)(2,1)}), bf16[3,2,96,384]{3,2,1,0:T(8,128)(2,1)}) %reduce-scatter.9.cloned.1.call-update) | async-done | bytes 442384 | tf_op jit(solution)/shard_map/reduce_scatter | solution.py:933
  676.6 98.3 %reduce-scatter.11.cloned.1.call-done = bf16[2,96,1536]{2,1,0:T(8,128)(2,1)} async-done(((bf16[2,768,1536]{2,1,0:T(8,128)(2,1)}), bf16[2,96,1536]{2,1,0:T(8,128)(2,1)}) %reduce-scatter.11.cloned.1.call-update) | async-done | bytes 589840 | tf_op jit(solution)/shard_map/reduce_scatter | solution.py:939
  775.0 3.3 add_convert_fusion
  783.0 14.8 %collective-permute-done.13 = bf16[512,768]{1,0:T(8,128)(2,1)S(1)} collective-permute-done((bf16[512,768]{1,0:T(8,128)(2,1)S(1)}, bf16[512,768]{1,0:T(8,128)(2,1)S(1)}, u32[]{:S(2)}, u32[]{:S(2)}) %collective-permute-start.13) | collective-permute-done | bytes 786464 | tf_op jit(solution)/shard_map/ppermute | solution.py:814
  798.7 41.3 %all-reduce.1 = (f32[6,768]{1,0:T(8,128)}, f32[2,32,12]{1,0,2:T(2,128)S(1)}) all-reduce(f32[6,768]{1,0:T(8,128)S(1)} %stack.153, f32[2,32,12]{1,0,2:T(2,128)S(1)} %copy_dynamic-update-slice_fusion), channel_id=1, replica_groups=mesh['dp'=2,'wide'=8,'narrow'=2] {'dp','wide','narrow'}, use_global_device_ids=true, to_apply=%region_32.33 | all-reduce | flops 5376 | bytes 43008 | tf_op jit(solution)/shard_map/psum | solution.py:959
  840.5 2.8 fusion.22
  843.3 2.3 convert_element_type.506
  (409 shorter events, 109.3 us)
Async XLA Ops:
  7.2 10.3 %copy-start.43 = (bf16[3,96,384]{2,1,0:T(8,128)(2,1)S(1)}, bf16[3,96,384]{2,1,0:T(8,128)(2,1)}, u32[]{:S(2)}) copy-start(bf16[3,96,384]{2,1,0:T(8,128)(2,1)} %param.17) | copy-start | bytes 663556
  7.2 450.6 %all-reduce.6.cloned.1.call-start = ((), (), s32[]{:S(2)}) async-start(), calls=%async_computation.8 | async-start | bytes 9437184
  10.9 135.1 %copy-start.55 = (bf16[128,768]{1,0:T(8,128)(2,1)}, bf16[128,768]{1,0:T(8,128)(2,1)S(1)}, u32[]{:S(2)}) copy-start(bf16[128,768]{1,0:T(8,128)(2,1)S(1)} %fusion.79) | copy-start | bytes 589828
  10.9 130.7 %collective-permute-start = (bf16[128,768]{1,0:T(8,128)(2,1)S(1)}, bf16[128,768]{1,0:T(8,128)(2,1)S(1)}, u32[]{:S(2)}, u32[]{:S(2)}) collective-permute-start(bf16[128,768]{1,0:T(8,128)(2,1)S(1)} %fusion.79), channel_id=1, source_target_pairs={{0,1},{1,0},{2,3},{3,2},{4,5},{5,4},{6,7},{7,6},{8,9},{9,8},{10,11... | collective-permute-start | bytes 589832 | tf_op jit(solution)/shard_map/ppermute | solution.py:808
  19.3 120.3 %copy-start.64 = (s32[4096]{0:T(1024)}, s32[4096]{0:T(1024)S(1)}, u32[]{:S(2)}) copy-start(s32[4096]{0:T(1024)S(1)} %compare_select_fusion.1) | copy-start | bytes 49156
  19.3 121.3 %copy-start.109 = (s32[1,4]{1,0:T(1,128)S(1)}, s32[1,4]{1,0:T(1,128)}, u32[]{:S(2)}) copy-start(s32[1,4]{1,0:T(1,128)} %param.16) | copy-start | bytes 52
  154.2 6.6 collective-permute-start.1
  161.2 5.7 collective-permute-start.2
  175.2 9.7 %copy-start.19 = (bf16[128,768]{1,0:T(8,128)(2,1)S(1)}, bf16[128,768]{1,0:T(8,128)(2,1)}, u32[]{:S(2)}) copy-start(bf16[128,768]{1,0:T(8,128)(2,1)} %param.25) | copy-start | bytes 589828
  176.8 6.2 collective-permute-start.3
  183.2 23.4 %copy-start.80 = (f32[128]{0:T(128)}, f32[128]{0:T(128)S(1)}, u32[]{:S(2)}) copy-start(f32[128]{0:T(128)S(1)} %fusion.103) | copy-start | bytes 1540
  183.3 5.7 collective-permute-start.4
  184.9 6.7 collective-permute-start.6
  198.0 7.8 collective-permute-start.7
  206.7 14.6 %copy-start.49 = (bf16[128,768]{1,0:T(8,128)(2,1)}, bf16[128,768]{1,0:T(8,128)(2,1)S(1)}, u32[]{:S(2)}) copy-start(bf16[128,768]{1,0:T(8,128)(2,1)S(1)} %fusion.118) | copy-start | bytes 589828
  206.7 5.7 collective-permute-start.8
  225.8 14.2 %copy-start.66 = (f32[768]{0:T(1024)S(1)}, f32[768]{0:T(1024)}, u32[]{:S(2)}) copy-start(f32[768]{0:T(1024)} %get-tuple-element.129) | copy-start | bytes 9220
  226.8 13.2 %collective-permute-start.9 = (bf16[512,768]{1,0:T(8,128)(2,1)}, bf16[512,768]{1,0:T(8,128)(2,1)}, u32[]{:S(2)}, u32[]{:S(2)}) collective-permute-start(bf16[512,768]{1,0:T(8,128)(2,1)} %constant_dynamic-slice_fusion.5), channel_id=1, source_target_pairs={{0,1},{1,0},{2,3},{3,2},{4,5},{5,4},{6,7},{7,6},{8,9},{9,8},{10,11... | collective-permute-start | bytes 2359304 | tf_op jit(solution)/shard_map/ppermute | solution.py:814
  227.7 15.2 %copy-start.13 = (bf16[512,768]{1,0:T(8,128)(2,1)S(1)}, bf16[512,768]{1,0:T(8,128)(2,1)}, u32[]{:S(2)}) copy-start(bf16[512,768]{1,0:T(8,128)(2,1)} %param.24) | copy-start | bytes 2359300
  246.1 12.0 %copy-start.17 = (bf16[512,768]{1,0:T(8,128)(2,1)}, bf16[512,768]{1,0:T(8,128)(2,1)S(1)}, u32[]{:S(2)}) copy-start(bf16[512,768]{1,0:T(8,128)(2,1)S(1)} %get-tuple-element.144) | copy-start | bytes 2359300
  246.1 12.0 %collective-permute-start.10 = (bf16[512,768]{1,0:T(8,128)(2,1)S(1)}, bf16[512,768]{1,0:T(8,128)(2,1)S(1)}, u32[]{:S(2)}, u32[]{:S(2)}) collective-permute-start(bf16[512,768]{1,0:T(8,128)(2,1)S(1)} %get-tuple-element.144), channel_id=1, source_target_pairs={{0,1},{1,0},{2,3},{3,2},{4,5},{5,4},{6,7},{7,6},{8,9},{9,8},{10,11... | collective-permute-start | bytes 2359304 | tf_op jit(solution)/shard_map/ppermute | solution.py:808
  247.2 11.7 %copy-start.119 = (bf16[1024,1536]{1,0:T(8,128)(2,1)S(1)}, bf16[1024,1536]{1,0:T(8,128)(2,1)}, u32[]{:S(2)}) copy-start(bf16[1024,1536]{1,0:T(8,128)(2,1)} %get-tuple-element.68) | copy-start | bytes 9437188
  277.2 249.1 %reduce-scatter.13.cloned.1.call-start = ((), (), s32[]{:S(2)}) async-start(), calls=%async_computation.7 | async-start | bytes 1990656
  290.8 22.9 %collective-permute-start.11 = (bf16[512,768]{1,0:T(8,128)(2,1)S(1)}, bf16[512,768]{1,0:T(8,128)(2,1)S(1)}, u32[]{:S(2)}, u32[]{:S(2)}) collective-permute-start(bf16[512,768]{1,0:T(8,128)(2,1)S(1)} %constant_dynamic-slice_fusion.4), channel_id=1, source_target_pairs={{0,1},{1,0},{2,3},{3,2},{4,5},{5,4},{6,7},{7,6},{8,9},{9,8},{10,11... | collective-permute-start | bytes 2359304 | tf_op jit(solution)/shard_map/ppermute | solution.py:814
  291.3 21.7 %copy-start.86 = (f32[128]{0:T(128)S(1)}, f32[128]{0:T(128)}, u32[]{:S(2)}) copy-start(f32[128]{0:T(128)} %copy-done.85) | copy-start | bytes 1540
  291.3 22.4 %copy-start.70 = (f32[512]{0:T(512)S(1)}, f32[512]{0:T(512)}, u32[]{:S(2)}) copy-start(f32[512]{0:T(512)} %fusion.99) | copy-start | bytes 6148
  291.3 21.7 %collective-permute-start.14 = (bf16[128,768]{1,0:T(8,128)(2,1)S(1)}, bf16[128,768]{1,0:T(8,128)(2,1)S(1)}, u32[]{:S(2)}, u32[]{:S(2)}) collective-permute-start(bf16[128,768]{1,0:T(8,128)(2,1)S(1)} %constant_dynamic-slice_fusion.2), channel_id=1, source_target_pairs={{0,1},{1,0},{2,3},{3,2},{4,5},{5,4},{6,7},{7,6},{8,9},{9,8},{10,11... | collective-permute-start | bytes 589832 | tf_op jit(solution)/shard_map/ppermute | solution.py:814
  293.0 20.7 %copy-start.3 = (f32[1024,768]{1,0:T(8,128)S(1)}, f32[1024,768]{1,0:T(8,128)}, u32[]{:S(2)}) copy-start(f32[1024,768]{1,0:T(8,128)} %get-tuple-element.52) | copy-start | bytes 9437188
  296.6 20.7 %collective-permute-start.5 = (bf16[128,768]{1,0:T(8,128)(2,1)S(1)}, bf16[128,768]{1,0:T(8,128)(2,1)S(1)}, u32[]{:S(2)}, u32[]{:S(2)}) collective-permute-start(bf16[128,768]{1,0:T(8,128)(2,1)S(1)} %constant_dynamic-slice_fusion.7), channel_id=1, source_target_pairs={{0,1},{1,0},{2,3},{3,2},{4,5},{5,4},{6,7},{7,6},{8,9},{9,8},{10,11... | collective-permute-start | bytes 589832 | tf_op jit(solution)/shard_map/ppermute | solution.py:814
  316.9 14.8 %copy-start.30 = (bf16[512,768]{1,0:T(8,128)(2,1)}, bf16[512,768]{1,0:T(8,128)(2,1)S(1)}, u32[]{:S(2)}) copy-start(bf16[512,768]{1,0:T(8,128)(2,1)S(1)} %get-tuple-element.142) | copy-start | bytes 2359300
  316.9 14.8 %collective-permute-start.12 = (bf16[512,768]{1,0:T(8,128)(2,1)S(1)}, bf16[512,768]{1,0:T(8,128)(2,1)S(1)}, u32[]{:S(2)}, u32[]{:S(2)}) collective-permute-start(bf16[512,768]{1,0:T(8,128)(2,1)S(1)} %get-tuple-element.142), channel_id=1, source_target_pairs={{0,1},{1,0},{2,3},{3,2},{4,5},{5,4},{6,7},{7,6},{8,9},{9,8},{10,11... | collective-permute-start | bytes 2359304 | tf_op jit(solution)/shard_map/ppermute | solution.py:808
  318.4 13.3 %copy-start.53 = (bf16[128,768]{1,0:T(8,128)(2,1)}, bf16[128,768]{1,0:T(8,128)(2,1)S(1)}, u32[]{:S(2)}) copy-start(bf16[128,768]{1,0:T(8,128)(2,1)S(1)} %get-tuple-element.140) | copy-start | bytes 589828
  318.4 12.9 %copy-start.21 = (bf16[256,384]{1,0:T(8,128)(2,1)S(1)}, bf16[256,384]{1,0:T(8,128)(2,1)}, u32[]{:S(2)}) copy-start(bf16[256,384]{1,0:T(8,128)(2,1)} %get-tuple-element.43.refs_4_) | copy-start | bytes 589828
  318.4 13.3 %copy-start.120 = (bf16[1024,384]{1,0:T(8,128)(2,1)S(1)}, bf16[1024,384]{1,0:T(8,128)(2,1)}, u32[]{:S(2)}) copy-start(bf16[1024,384]{1,0:T(8,128)(2,1)} %get-tuple-element.55.refs_4_) | copy-start | bytes 2359300
  318.4 12.9 %collective-permute-start.15 = (bf16[128,768]{1,0:T(8,128)(2,1)S(1)}, bf16[128,768]{1,0:T(8,128)(2,1)S(1)}, u32[]{:S(2)}, u32[]{:S(2)}) collective-permute-start(bf16[128,768]{1,0:T(8,128)(2,1)S(1)} %get-tuple-element.140), channel_id=1, source_target_pairs={{0,1},{1,0},{2,3},{3,2},{4,5},{5,4},{6,7},{7,6},{8,9},{9,8},{10,11... | collective-permute-start | bytes 589832 | tf_op jit(solution)/shard_map/ppermute | solution.py:808
  339.5 255.6 %reduce-scatter.7.cloned.1.call-start = ((), (), s32[]{:S(2)}) async-start(), calls=%async_computation.4 | async-start | bytes 1990656 | tf_op jit(solution)/shard_map/reduce_scatter | solution.py:930
  384.3 292.3 %reduce-scatter.9.cloned.1.call-start = ((), (), s32[]{:S(2)}) async-start(), calls=%async_computation.5 | async-start | bytes 3981312 | tf_op jit(solution)/shard_map/reduce_scatter | solution.py:933
  396.7 378.2 %reduce-scatter.11.cloned.1.call-start = ((), (), s32[]{:S(2)}) async-start(), calls=%async_computation.6 | async-start | bytes 5308416 | tf_op jit(solution)/shard_map/reduce_scatter | solution.py:939
  406.7 436.6 %all-reduce.8.cloned.1.call-start = ((), (), s32[]{:S(2)}) async-start(), calls=%async_computation.9 | async-start | bytes 4276224 | tf_op jit(solution)/shard_map/psum | solution.py:949
  413.4 5.7 collective-permute-start.16
  778.3 19.5 %copy-start = (bf16[1024,768]{1,0:T(8,128)(2,1)}, bf16[1024,768]{1,0:T(8,128)(2,1)S(1)}, u32[]{:S(2)}) copy-start(bf16[1024,768]{1,0:T(8,128)(2,1)S(1)} %add_convert_fusion) | copy-start | bytes 4718596
  778.5 19.3 %copy-start.5 = (bf16[512,768]{1,0:T(8,128)(2,1)S(1)}, bf16[512,768]{1,0:T(8,128)(2,1)}, u32[]{:S(2)}) copy-start(bf16[512,768]{1,0:T(8,128)(2,1)} %x_own.1) | copy-start | bytes 2359300
  778.5 19.3 %copy-start.67 = (f32[768]{0:T(1024)S(1)}, f32[768]{0:T(1024)}, u32[]{:S(2)}) copy-start(f32[768]{0:T(1024)} %get-tuple-element.127) | copy-start | bytes 9220
  778.5 19.3 %collective-permute-start.13 = (bf16[512,768]{1,0:T(8,128)(2,1)S(1)}, bf16[512,768]{1,0:T(8,128)(2,1)S(1)}, u32[]{:S(2)}, u32[]{:S(2)}) collective-permute-start(bf16[512,768]{1,0:T(8,128)(2,1)S(1)} %constant_dynamic-slice_fusion.3), channel_id=1, source_target_pairs={{0,1},{1,0},{2,3},{3,2},{4,5},{5,4},{6,7},{7,6},{8,9},{9,8},{10,11... | collective-permute-start | bytes 2359304 | tf_op jit(solution)/shard_map/ppermute | solution.py:814
  781.9 16.7 %copy-start.77 = (f32[1,768]{1,0:T(1,128)S(1)}, f32[1,768]{1,0:T(1,128)}, u32[]{:S(2)}) copy-start(f32[1,768]{1,0:T(1,128)} %reshape.342) | copy-start | bytes 9220
  781.9 16.7 %copy-start.78 = (f32[1,768]{1,0:T(1,128)S(1)}, f32[1,768]{1,0:T(1,128)}, u32[]{:S(2)}) copy-start(f32[1,768]{1,0:T(1,128)} %reshape.341) | copy-start | bytes 9220
  781.9 16.7 %copy-start.79 = (f32[1,768]{1,0:T(1,128)S(1)}, f32[1,768]{1,0:T(1,128)}, u32[]{:S(2)}) copy-start(f32[1,768]{1,0:T(1,128)} %reshape.340) | copy-start | bytes 9220
  781.9 58.6 %copy-start.6 = (f32[512,768]{1,0:T(8,128)S(1)}, f32[512,768]{1,0:T(8,128)}, u32[]{:S(2)}) copy-start(f32[512,768]{1,0:T(8,128)} %get-tuple-element.143) | copy-start | bytes 4718596
  (96 other events, 342.7 us)
Sparse Core Ops, SparseCore 0:
  277.3 180.3 all-reduce.5
  461.2 65.0 reduce-scatter.12
  530.2 64.8 reduce-scatter.6
  598.6 77.9 reduce-scatter.8
  680.1 94.7 reduce-scatter.10
  778.6 21.2 all-reduce.7

commit v2 on v1

--- a/solution.py
+++ b/solution.py
@@ -762,6 +762,566 @@
     return pull(grad_normed)
 
 
+NEAR = 2 * CHUNK
+
+
+def norm_back(values, gain, grad):
+    scale = lax.rsqrt(jnp.mean(values * values, axis=1, keepdims=True) + EPS)
+    scaled = grad * gain
+    pulled = scale * (scaled - values * (scale * scale) * jnp.mean(scaled * values, axis=1, keepdims=True))
+    return pulled, jnp.sum(grad * values * scale, axis=0, keepdims=True)
+
+
+class Scatter:
+    def __init__(self, place, rows, groups, tile, send, receive):
+        self.place, self.rows, self.groups, self.tile = place, rows, groups, tile
+        self.send, self.receive = send, receive
+        self.sent = []
+
+    def columns(self, group, core):
+        first, width = self.groups[group]["first"], self.groups[group]["width"]
+        return pl.ds(pl.multiple_of(first + core * (width // 2), 128), width // 2)
+
+    def block(self, group, index):
+        return self.groups[group]["grad"].at[
+            pl.ds(pl.multiple_of(index * self.rows, 16), self.rows), self.columns(group, self.place.core)
+        ]
+
+    def push(self, group, slot, source, target, partner, arrival=None):
+        arrival = slot if arrival is None else arrival
+        copy = remote(source, target, self.send.at[group, slot], self.receive.at[group, arrival], partner)
+        copy.start()
+        self.sent.append(copy)
+
+    def await_slot(self, group, slot, block):
+        remote(block, block, self.send.at[group, 0], self.receive.at[group, slot], self.place.sibling()).wait_recv()
+
+    def start(self, group):
+        parts = self.groups[group]
+        self.push(
+            group, 0, parts["grad"].at[:, self.columns(group, 1 - self.place.core)], parts["core"], self.place.sibling()
+        )
+
+    def add_block(self, group, index, other):
+        block = self.block(group, index)
+        block[...] = (block[...].astype(jnp.float32) + other.astype(jnp.float32)).astype(jnp.bfloat16)
+        return block
+
+    def beside(self, group):
+        parts, place = self.groups[group], self.place
+        self.await_slot(group, 0, parts["core"])
+
+        def received(index):
+            return parts["core"][pl.ds(pl.multiple_of(index * self.rows, 16), self.rows), :]
+
+        for step in range(place.fars):
+            far = lax.rem(place.far + 1 + step, place.fars)
+            index = 2 * far + 1 - place.near
+            block = self.add_block(group, index, received(index))
+            self.push(group, 1 + step, block, parts["beside"].at[step], place.beside())
+        for step in range(place.fars):
+            far = lax.rem(place.far + 1 + step, place.fars)
+            index = 2 * far + place.near
+            self.add_block(group, index, received(index))
+
+    def along(self, group):
+        parts, place = self.groups[group], self.place
+        for step in range(1, place.fars):
+            index = 2 * lax.rem(place.far + step, place.fars) + place.near
+            self.await_slot(group, step, parts["beside"].at[step - 1])
+            block = self.add_block(group, index, parts["beside"][step - 1])
+            self.push(group, place.fars + step, block, parts["along"].at[step - 1], place.along(step))
+
+    def total(self, group):
+        parts, place = self.groups[group], self.place
+        self.await_slot(group, place.fars, parts["beside"].at[place.fars - 1])
+        value = self.block(group, place.wide)[...].astype(jnp.float32) + parts["beside"][place.fars - 1].astype(jnp.float32)
+        for step in range(1, place.fars):
+            self.await_slot(group, place.fars + step, parts["along"].at[step - 1])
+            value = value + parts["along"][step - 1].astype(jnp.float32)
+        half = parts["width"] // 2
+        block = self.tile.at[:, pl.ds(pl.multiple_of(parts["out"] + place.core * half, 128), half)]
+        block[...] = value.astype(jnp.bfloat16)
+        self.push(group, 2 * place.fars, block, block, place.sibling())
+
+    def finish(self, group):
+        parts, place = self.groups[group], self.place
+        half = parts["width"] // 2
+        block = self.tile.at[:, pl.ds(pl.multiple_of(parts["out"] + (1 - place.core) * half, 128), half)]
+        self.await_slot(group, 2 * place.fars, block)
+
+    def close(self):
+        for copy in self.sent:
+            copy.wait_send()
+
+
+def scatter_slots(wide):
+    return 2 * (wide // 2) + 1
+
+
+def scatter_buffers(wide, model, width):
+    half, rows, fars = width // 2, model // wide, wide // 2
+    return [
+        pltpu.VMEM((model, half), jnp.bfloat16),
+        pltpu.VMEM((fars, rows, half), jnp.bfloat16),
+        pltpu.VMEM((fars - 1, rows, half), jnp.bfloat16),
+    ]
+
+
+def softmax_back_pair(q_pair, k_pair, v_pair, c_pair, inverse, gc_pair, weights, near):
+    scaled = (gc_pair.astype(jnp.float32) * inverse).astype(jnp.bfloat16)
+    product = scaled.astype(jnp.float32) * c_pair.astype(jnp.float32)
+    lane = lax.broadcasted_iota(jnp.int32, product.shape, 1)
+    inner = (
+        jnp.sum(jnp.where(lane < DK, product, 0.0), axis=1, keepdims=True),
+        jnp.sum(jnp.where(lane < DK, 0.0, product), axis=1, keepdims=True),
+    )
+    g_heads = split_heads(scaled)
+    q_heads = split_heads(q_pair)
+    k_heads = split_heads(k_pair)
+    gq = None
+    grads = []
+    for head in range(2):
+        grad = weights[head].astype(jnp.float32) * (dot_nt(g_heads[head], v_pair) - inner[head])
+        if near is not None:
+            near(head, grad)
+        grad = grad.astype(jnp.bfloat16)
+        grads.append(grad)
+        part = dot_nn(grad, k_heads[head])
+        gq = part if gq is None else gq + part
+    gk = dot_tn(jnp.concatenate(grads, axis=0), jnp.concatenate(q_heads, axis=0))
+    gv = dot_tn(jnp.concatenate([weights[0], weights[1]], axis=0), jnp.concatenate(g_heads, axis=0))
+    return gq, gk, gv
+
+
+def fold_near(rows):
+    total = jnp.zeros((8, 2 * NEAR), jnp.float32)
+    blank = jnp.zeros((8, NEAR), jnp.float32)
+    for a in range(CHUNK // 8):
+        wider = jnp.concatenate([rows[8 * a : 8 * a + 8, :], blank], axis=1)
+        total = total + pltpu.roll(wider, (CHUNK - 8 * a) % (2 * NEAR), 1)
+    return total
+
+
+def near_table_grad(near_sums, far_sums):
+    heads = near_sums.shape[0]
+    places = jnp.arange(2 * NEAR, dtype=jnp.int32)[None, :]
+    relative = places - jnp.arange(8, dtype=jnp.int32)[:, None] - CHUNK - NEAR // 4
+    buckets = bucket_index(relative.reshape(-1), True)
+    onehot = (buckets[None, :] == jnp.arange(NB, dtype=jnp.int32)[:, None]).astype(jnp.float32)
+    near = lax.dot_general(
+        onehot,
+        near_sums.reshape(heads, 16 * NEAR),
+        (((1,), (1,)), ((), ())),
+        precision=HIGH,
+        preferred_element_type=jnp.float32,
+    )
+    far = jnp.sum(far_sums, axis=(2, 3))
+    ends = jnp.array([[NB // 2 - 1], [NB - 1]], jnp.int32)
+    choose = (ends == jnp.arange(NB, dtype=jnp.int32)[None, :]).astype(jnp.float32)
+    return near + lax.dot_general(choose, far, (((0,), (0,)), ((), ())), precision=HIGH, preferred_element_type=jnp.float32)
+
+
+def enc_backward_kernel(
+    wide,
+    x_own,
+    cot_own,
+    cot_other,
+    gains,
+    memory_part,
+    w1_in,
+    n0_in,
+    qkv_in,
+    c_in,
+    inv_in,
+    e_all,
+    e1_all,
+    n1_in,
+    slope_all,
+    a_in,
+    ef_all,
+    grad_out,
+    tile,
+    gain_sums,
+    near_sums,
+    far_sums,
+    w1,
+    n0,
+    qkv,
+    c,
+    inv,
+    n1,
+    active,
+    cot,
+    e_buf,
+    state_buf,
+    slope_buf,
+    part_buf,
+    m_recv,
+    g_send,
+    g_recv,
+    state_grad,
+    gy,
+    gu,
+    gqkv,
+    gk_sum,
+    gv_sum,
+    strip,
+    core_f,
+    beside_f,
+    along_f,
+    beside_a,
+    along_a,
+    s_send,
+    s_recv,
+    m_sems,
+    g_sems,
+    l_sems,
+    e_sems,
+    t_sems,
+    i_sems,
+):
+    place = Place(wide)
+    side = place.side
+    half = x_own.shape[0]
+    rows = 2 * half
+    steps = rows // CHUNK
+    width = c.shape[1]
+    ffn = active.shape[1]
+    pairs = width // PAIR
+    model = x_own.shape[1]
+    bf, f32 = jnp.bfloat16, jnp.float32
+    place.greet()
+
+    def swap(kind, i):
+        at = pl.ds(i * CHUNK, CHUNK)
+        if kind == 0:
+            return remote(memory_part.at[at], m_recv.at[at], m_sems.at[0, i], m_sems.at[1, i], place.across())
+        return remote(g_send.at[at], g_recv.at[at], g_sems.at[0, i], g_sems.at[1, i], place.across())
+
+    for i in range(steps):
+        swap(0, i).start()
+
+    def fetch(i):
+        at = pl.ds(i * CHUNK, CHUNK)
+        slot = i % 2
+        return [
+            pltpu.make_async_copy(ef_all.at[at], state_buf.at[slot], t_sems.at[0, slot]),
+            pltpu.make_async_copy(slope_all.at[at], slope_buf.at[slot], t_sems.at[1, slot]),
+            pltpu.make_async_copy(memory_part.at[at], part_buf.at[slot], t_sems.at[2, slot]),
+        ]
+
+    def fetch_state(i):
+        at = pl.ds(i * CHUNK, CHUNK)
+        return pltpu.make_async_copy(e1_all.at[at], state_buf.at[i % 2], t_sems.at[0, i % 2])
+
+    def fetch_e(step):
+        chunk, pair, slot = step // pairs, lax.rem(step, pairs), lax.rem(step, 2)
+        at = pl.ds(pl.multiple_of(chunk * CHUNK, CHUNK), CHUNK)
+        return pltpu.make_async_copy(e_all.at[pl.ds(2 * pair, 2), at, :], e_buf.at[slot], e_sems.at[slot])
+
+    mine = pl.ds(pl.multiple_of(side * half, 16), half)
+    theirs = pl.ds(pl.multiple_of((1 - side) * half, 16), half)
+    loads = [
+        pltpu.make_async_copy(cot_own, cot.at[mine], i_sems.at[0]),
+        pltpu.make_async_copy(cot_other, cot.at[theirs], i_sems.at[1]),
+        pltpu.make_async_copy(w1_in, w1, i_sems.at[2]),
+        pltpu.make_async_copy(a_in, active, i_sems.at[3]),
+        pltpu.make_async_copy(n1_in, n1, i_sems.at[4]),
+        pltpu.make_async_copy(qkv_in, qkv, i_sems.at[5]),
+        pltpu.make_async_copy(c_in, c, i_sems.at[6]),
+        pltpu.make_async_copy(inv_in, inv, i_sems.at[7]),
+        pltpu.make_async_copy(n0_in, n0, i_sems.at[8]),
+    ]
+    for load in loads[:2]:
+        load.start()
+    for load in fetch(0):
+        load.start()
+    for load in loads[2:]:
+        load.start()
+    gk_sum[...] = jnp.zeros_like(gk_sum)
+    gv_sum[...] = jnp.zeros_like(gv_sum)
+    strip[...] = jnp.zeros_like(strip)
+    far_sums[...] = jnp.zeros_like(far_sums)
+    gain_sums[...] = jnp.zeros_like(gain_sums)
+    scatter = Scatter(
+        place,
+        model // wide,
+        [
+            dict(grad=w1, first=4 * width, width=2 * ffn, out=4 * width, core=core_f, beside=beside_f, along=along_f),
+            dict(grad=gu.at[pl.ds(0, model)], first=0, width=4 * width, out=0, core=active.at[pl.ds(0, model), pl.ds(0, 2 * width)], beside=beside_a, along=along_a),
+        ],
+        tile,
+        s_send,
+        s_recv,
+    )
+
+    def own_weight(i):
+        return jnp.where((i * CHUNK) // half == side, 1.0, 0.0).astype(f32)
+
+    for load in loads[:3]:
+        load.wait()
+
+    for i in range(steps):
+        at = slice(i * CHUNK, (i + 1) * CHUNK)
+        slot = i % 2
+        if i + 1 < steps:
+            for load in fetch(i + 1):
+                load.start()
+        for load in fetch(i):
+            load.wait()
+        swap(0, i).wait_recv()
+        grad = part_buf[slot].astype(f32) + m_recv[at, :].astype(f32)
+        pulled, gain = norm_back(state_buf[slot], gains[5:6, :], grad)
+        gain_sums[5:6, :] += gain * own_weight(i)
+        total = cot[at, :].astype(f32) + pulled
+        state_grad[at, :] = total
+        gy[at, :] = total.astype(bf)
+
+        def part(j, carry):
+            cols = pl.ds(pl.multiple_of(4 * width + ffn + j * width, PAIR), width)
+            here = pl.ds(pl.multiple_of(j * width, PAIR), width)
+            grad_active = dot_nn(gy[at, :], w1[:, cols])
+            gu[at, here] = (slope_buf[slot, :, here].astype(f32) * grad_active).astype(bf)
+            return carry
+
+        lax.fori_loop(0, ffn // width, part, 0)
+        g_send[at, :] = dot_nt(gu[at, :], w1[:, 4 * width : 4 * width + ffn]).astype(bf)
+        swap(1, i).start()
+    for load in loads[3:]:
+        load.wait()
+    fetch_state(0).start()
+    fetch_e(0).start()
+
+    def weight_grads(t, carry):
+        tile_rows = pl.ds(pl.multiple_of(t * CHUNK, CHUNK), CHUNK)
+        w1[tile_rows, 4 * width : 4 * width + ffn] = dot_tn(n1[:, tile_rows], gu[...]).astype(bf)
+        w1[tile_rows, 4 * width + ffn :] = dot_tn(gy[:, tile_rows], active[...]).astype(bf)
+        return carry
+
+    lax.fori_loop(0, model // CHUNK, weight_grads, 0)
+    scatter.start(0)
+
+    dw0 = gu
+    l_send, l_recv = n1, m_recv
+
+    def lanes(base_lane, pair):
+        return pl.ds(pl.multiple_of(base_lane + pair * PAIR, PAIR), PAIR)
+
+    def attend_back(i):
+        at = slice(i * CHUNK, (i + 1) * CHUNK)
+        slot = i % 2
+        if i + 1 < steps:
+            fetch_state(i + 1).start()
+        fetch_state(i).wait()
+        swap(1, i).wait_recv()
+        grad = g_send[at, :].astype(f32) + g_recv[at, :].astype(f32)
+        pulled, gain = norm_back(state_buf[slot], gains[1:2, :], grad)
+        gain_sums[1:2, :] += gain * own_weight(i)
+        total = state_grad[at, :] + pulled
+        state_grad[at, :] = total
+        gy[at, :] = total.astype(bf)
+        g_send[at, :width] = dot_nn(gy[at, :], w1[:, 3 * width : 4 * width]).astype(bf)
+        low, high = max(i * CHUNK - NEAR // 4, 0), min(i * CHUNK + CHUNK + NEAR // 4, rows)
+        shift = low - (i * CHUNK - NEAR // 4)
+
+        def one(pair, carry):
+            step = i * pairs + pair
+
+            @pl.when(step + 1 < steps * pairs)
+            def _():
+                fetch_e(step + 1).start()
+
+            fetch_e(step).wait()
+            e_slot = lax.rem(step, 2)
+
+            def near(head, grad):
+                strip[2 * pair + head, :, shift : shift + high - low] += grad[:, low:high]
+                for edge, (start, end) in enumerate(((0, low), (high, rows))):
+                    if end > start:
+                        folded = jnp.sum(grad[:, start:end].reshape(CHUNK // 8, 8, end - start), axis=0)
+                        wide_sum = folded[:, :128]
+                        for lane in range(128, end - start, 128):
+                            wide_sum = wide_sum + folded[:, lane : lane + 128]
+                        far_sums[edge, 2 * pair + head] += wide_sum
+
+            gq, gk, gv = softmax_back_pair(
+                qkv[at, lanes(0, pair)],
+                qkv[:, lanes(width, pair)],
+                qkv[:, lanes(2 * width, pair)],
+                c[at, lanes(0, pair)],
+                inv[at, lanes(0, pair)],
+                g_send[at, lanes(0, pair)],
+                (e_buf[e_slot, 0], e_buf[e_slot, 1]),
+                near,
+            )
+            gqkv[at, lanes(0, pair)] = gq.astype(bf)
+            gk_sum[:, lanes(0, pair)] += gk
+            gv_sum[:, lanes(0, pair)] += gv
+            return carry
+
+        lax.fori_loop(0, pairs, one, 0)
+
+    for i in range(steps):
+        swap(1, i).wait_send()
+        attend_back(i)
+        if i == 0:
+            scatter.beside(0)
+        if i == 2:
+            scatter.along(0)
+    gqkv[:, width : 2 * width] = gk_sum[...].astype(bf)
+    gqkv[:, 2 * width :] = gv_sum[...].astype(bf)
+
+    def weight_grads_a(t, carry):
+        tile_rows = pl.ds(pl.multiple_of(t * CHUNK, CHUNK), CHUNK)
+        dw0[tile_rows, : 3 * width] = dot_tn(n0[:, tile_rows], gqkv[...]).astype(bf)
+        dw0[tile_rows, 3 * width :] = dot_tn(gy[:, tile_rows], c[...]).astype(bf)
+        return carry
+
+    lax.fori_loop(0, model // CHUNK, weight_grads_a, 0)
+    scatter.start(1)
+    last = []
+    for part in range(half // CHUNK):
+        there = pl.ds(pl.multiple_of((1 - side) * half + part * CHUNK, CHUNK), CHUNK)
+        at = pl.ds(part * CHUNK, CHUNK)
+        l_send[at, :] = dot_nt(gqkv[there, :], w1[:, : 3 * width]).astype(bf)
+        last.append(remote(l_send.at[at], l_recv.at[at], l_sems.at[0, part], l_sems.at[1, part], place.across()))
+        last[part].start()
+        if part == 0:
+            scatter.beside(1)
+    scatter.total(0)
+
+    def fold(head, carry):
+        near_sums[head] = fold_near(strip[head])
+        return carry
+
+    lax.fori_loop(0, 2 * pairs, fold, 0)
+    scatter.along(1)
+    for part in range(half // CHUNK):
+        here = pl.ds(pl.multiple_of(side * half + part * CHUNK, CHUNK), CHUNK)
+        at = pl.ds(part * CHUNK, CHUNK)
+        own = dot_nt(gqkv[here, :], w1[:, : 3 * width])
+        last[part].wait_recv()
+        grad = own + l_recv[at, :].astype(f32)
+        pulled, gain = norm_back(x_own[at, :].astype(f32), gains[0:1, :], grad)
+        gain_sums[0:1, :] += gain
+        grad_out[at, :] = state_grad[here, :] + pulled
+    scatter.total(1)
+    scatter.finish(0)
+    scatter.finish(1)
+    scatter.close()
+    for i in range(steps):
+        swap(0, i).wait_send()
+    for copy in last:
+        copy.wait_send()
+
+
+def enc_backward(wide, x_own, cot_own, cot_other, gains, memory_part, saved):
+    half, model = x_own.shape
+    rows = 2 * half
+    w1, n0, qkv, c, inv, e_all, e1, n1, slope, active, ef = saved
+    width, ffn = c.shape[1], active.shape[1]
+    pairs = width // PAIR
+    steps = rows // CHUNK
+    bf, f32 = jnp.bfloat16, jnp.float32
+    shape = jax.ShapeDtypeStruct
+    dma = pltpu.SemaphoreType.DMA
+    return pl.pallas_call(
+        functools.partial(enc_backward_kernel, wide),
+        in_specs=[vmem_spec(), any_spec(), any_spec(), vmem_spec()] + [any_spec()] * 12,
+        out_shape=[
+            shape((half, model), f32),
+            shape((model // wide, 4 * width + 2 * ffn), bf),
+            shape((8, model), f32),
+            shape((2 * pairs, 8, 2 * NEAR), f32),
+            shape((2, 2 * pairs, 8, 128), f32),
+        ],
+        out_specs=[vmem_spec()] * 5,
+        scratch_shapes=[
+            pltpu.VMEM(w1.shape, bf),
+            pltpu.VMEM(n0.shape, bf),
+            pltpu.VMEM(qkv.shape, bf),
+            pltpu.VMEM(c.shape, bf),
+            pltpu.VMEM(inv.shape, f32),
+            pltpu.VMEM(n1.shape, bf),
+            pltpu.VMEM(active.shape, bf),
+            pltpu.VMEM((rows, model), bf),
+            pltpu.VMEM((2, 2, CHUNK, rows), bf),
+            pltpu.VMEM((2, CHUNK, model), f32),
+            pltpu.VMEM((2, CHUNK, ffn), bf),
+            pltpu.VMEM((2, CHUNK, model), bf),
+            pltpu.VMEM((rows, model), bf),
+            pltpu.VMEM((rows, model), bf),
+            pltpu.VMEM((rows, model), bf),
+            pltpu.VMEM((rows, model), f32),
+            pltpu.VMEM((rows, model), bf),
+            pltpu.VMEM((rows, ffn), bf),
+            pltpu.VMEM((rows, 3 * width), bf),
+            pltpu.VMEM((rows, width), f32),
+            pltpu.VMEM((rows, width), f32),
+            pltpu.VMEM((2 * pairs, CHUNK, NEAR), f32),
+        ]
+        + scatter_buffers(wide, model, 2 * ffn)
+        + scatter_buffers(wide, model, 4 * width)[1:]
+        + [
+            dma((2, scatter_slots(wide))),
+            dma((2, scatter_slots(wide))),
+            dma((2, steps)),
+            dma((2, steps)),
+            dma((2, half // CHUNK)),
+            dma((2,)),
+            dma((3, 2)),
+            dma((9,)),
+        ],
+        compiler_params=pltpu.CompilerParams(
+            collective_id=1, has_side_effects=True, vmem_limit_bytes=VMEM_BYTES
+        ),
+        cost_estimate=pl.CostEstimate(flops=2 * 10**10, bytes_accessed=6 * 10**7, transcendentals=0),
+    )(x_own, cot_own, cot_other, gains, memory_part, w1, n0, qkv, c, inv, e_all, e1, n1, slope, active, ef)
+
+
+def scatter_kernel(wide, widths, grad_in, tile, grad, *refs):
+    place = Place(wide)
+    place.greet()
+    load = pltpu.make_async_copy(grad_in, grad, refs[-1].at[0])
+    load.start()
+    groups = []
+    first = 0
+    for index, width in enumerate(widths):
+        core, beside, along = refs[3 * index : 3 * index + 3]
+        groups.append(dict(grad=grad, first=first, width=width, out=first, core=core, beside=beside, along=along))
+        first += width
+    scatter = Scatter(place, tile.shape[0], groups, tile, refs[-3], refs[-2])
+    load.wait()
+    count = len(widths)
+    for group in range(count):
+        scatter.start(group)
+    for stage in (scatter.beside, scatter.along, scatter.total, scatter.finish):
+        for group in range(count):
+            stage(group)
+    scatter.close()
+
+
+def scatter_grads(wide, grad, widths):
+    model, total = grad.shape
+    buffers = []
+    for width in widths:
+        buffers += scatter_buffers(wide, model, width)
+    dma = pltpu.SemaphoreType.DMA
+    return pl.pallas_call(
+        functools.partial(scatter_kernel, wide, widths),
+        in_specs=[any_spec()],
+        out_shape=jax.ShapeDtypeStruct((model // wide, total), jnp.bfloat16),
+        out_specs=vmem_spec(),
+        scratch_shapes=[pltpu.VMEM((model, total), jnp.bfloat16)]
+        + buffers
+        + [dma((len(widths), scatter_slots(wide))), dma((len(widths), scatter_slots(wide))), dma((1,))],
+        compiler_params=pltpu.CompilerParams(
+            collective_id=2, has_side_effects=True, vmem_limit_bytes=VMEM_BYTES
+        ),
+    )(grad)
+
+
 def pack_shards(attn_query, attn_kv, attn_out, ffn_up, ffn_down):
     def attention(layer):
         return [attn_query[layer], attn_kv[layer, 0], attn_kv[layer, 1], attn_out[layer].T]
@@ -823,6 +1383,7 @@
         parts = dot_nt(saved[1], weights_o[layer])
         return ((query, keys, values, saved), collect_rows(parts))
 
+    cot_other = lax.ppermute(enc_cotangent, "narrow", swap)
     pack = pack_shards(attn_query, attn_kv, attn_out, ffn_up, ffn_down)
     w1, w2, rows_a, qkv_a, context_a, inverse_a, e_a, e1_full, rows_b, slope_b, active_b, ef_full, memory = enc_forward(
         wide, enc_input, pack, gain_rows, base_rows(rel_bias[0], ENC, True), enc_segments
@@ -836,20 +1397,12 @@
     weights_o = [columns[:, 3 * width :] for columns in layer_columns]
     up = [w1[:, 4 * width : 4 * width + ffn], w2[:, 8 * width : 8 * width + ffn]]
     down = [w1[:, 4 * width + ffn :], w2[:, 8 * width + ffn :]]
-    kept_a = (
-        qkv_a[:, :width],
-        qkv_a[:, width : 2 * width],
-        qkv_a[:, 2 * width :],
-        (e_a, context_a, inverse_a),
-    )
     half = enc_input.shape[0]
 
     def own_rows(full):
         return lax.dynamic_slice_in_dim(full, side * half, half)
 
-    enc_start = enc_input.astype(jnp.float32)
-    enc_mid = own_rows(e1_full)
-    enc_final = own_rows(ef_full)
+    enc_output = own_rows(ef_full).astype(jnp.bfloat16)
     dec_start = dec_input.astype(jnp.float32)
     rows_c = spread_rows(rms_norm(dec_start, gain_rows[2]))
     kept_c, branch = attention_layer(
@@ -894,7 +1447,7 @@
     query_part, memory_part, sums_d = attention_back(
         grad_dec, kept_d, rows_d, memory, 2, 0, False
     )
-    grad_normed, grad_memory = collect_rows(query_part), collect_rows(memory_part)
+    grad_normed = collect_rows(query_part)
     grad_back, gain_d = norm_backward(dec_one, gain_rows[3], grad_normed)
     grad_dec = grad_dec + grad_back
     query_part, key_part, sums_c = attention_back(
@@ -902,72 +1455,46 @@
     )
     grad_back, gain_c = norm_backward(dec_start, gain_rows[2], collect_rows(query_part + key_part))
     grad_dec = grad_dec + grad_back
-    grad_enc = enc_cotangent.astype(jnp.float32)
-    grad_back, gain_m = norm_backward(enc_final, gain_rows[5], grad_memory)
-    grad_enc = grad_enc + grad_back
-    grad_normed, up_b, down_b = ffn_back(
-        spread_rows(grad_enc), rows_b, slope_b, active_b, up[0], down[0]
-    )
-    grad_back, gain_b = norm_backward(enc_mid, gain_rows[1], collect_rows(grad_normed))
-    grad_enc = grad_enc + grad_back
-    query_part, key_part, sums_a = attention_back(
-        grad_enc, kept_a, rows_a, rows_a, 0, ENC, True
-    )
-    grad_back, gain_a = norm_backward(enc_start, gain_rows[0], collect_rows(query_part + key_part))
-    grad_enc = grad_enc + grad_back
-    grad_query = jnp.stack([sums_a[0], sums_c[0], sums_d[0]])
+    grad_dec_query = jnp.concatenate([sums_c[0], sums_c[1], sums_c[2], sums_c[3].T, sums_d[0], sums_d[1], sums_d[2], sums_d[3].T, up_e, down_e.T], axis=1)
+    grad_enc, tile_one, gain_sums, near_sums, far_sums = enc_backward(
+        wide,
+        enc_input,
+        enc_cotangent,
+        cot_other,
+        gain_rows,
+        memory_part.astype(jnp.bfloat16),
+        (w1, rows_a, qkv_a, context_a, inverse_a, e_a, e1_full, rows_b, slope_b, active_b, ef_full),
+    )
+    tile_two = scatter_grads(wide, grad_dec_query.astype(jnp.bfloat16), (2 * ffn, 4 * width, 4 * width))
+    tile_one, tile_two = tile_one.astype(jnp.float32), tile_two.astype(jnp.float32)
+    at_a, at_c, at_d = tile_one[:, : 4 * width], tile_two[:, : 4 * width], tile_two[:, 4 * width : 8 * width]
+    layers = (at_a, at_c, at_d)
+    feeds = (tile_one[:, 4 * width :], tile_two[:, 8 * width :])
+    grad_query = jnp.stack([layer[:, :width] for layer in layers])
     grad_kv = jnp.stack(
-        [
-            jnp.stack([sums_a[1], sums_a[2]]),
-            jnp.stack([sums_c[1], sums_c[2]]),
-            jnp.stack([sums_d[1], sums_d[2]]),
-        ]
-    )
-    grad_out = jnp.stack([sums_a[3], sums_c[3], sums_d[3]])
-    grad_up = jnp.stack([up_b, up_e])
-    grad_down = jnp.stack([down_b, down_e])
-    tiles = (
-        lax.psum_scatter(
-            grad_query.astype(jnp.bfloat16), "wide", scatter_dimension=1, tiled=True
-        ).astype(jnp.float32),
-        lax.psum_scatter(
-            grad_kv.astype(jnp.bfloat16), "wide", scatter_dimension=2, tiled=True
-        ).astype(jnp.float32),
-        lax.psum_scatter(
-            grad_out.astype(jnp.bfloat16), "wide", scatter_dimension=2, tiled=True
-        ).astype(jnp.float32),
-        lax.psum_scatter(
-            grad_up.astype(jnp.bfloat16), "wide", scatter_dimension=1, tiled=True
-        ).astype(jnp.float32),
-        lax.psum_scatter(
-            grad_down.astype(jnp.bfloat16), "wide", scatter_dimension=2, tiled=True
-        ).astype(jnp.float32),
-    )
-    tiles = (
-        lax.psum(tiles[0].astype(jnp.bfloat16), "dp").astype(jnp.float32),
-        lax.psum(tiles[1].astype(jnp.bfloat16), "dp").astype(jnp.float32),
-        lax.psum(tiles[2].astype(jnp.bfloat16), "dp").astype(jnp.float32),
-        lax.psum(tiles[3].astype(jnp.bfloat16), "dp").astype(jnp.float32),
-        lax.psum(tiles[4].astype(jnp.bfloat16), "dp").astype(jnp.float32),
-    )
-    gain_grads = jnp.stack([gain_a, gain_b, gain_c, gain_d, gain_e, gain_m])
-    column = lax.axis_index("narrow") * heads_local
-    bias_local = jnp.stack([sums_a[4], sums_c[4]])
-    bias_full = lax.dynamic_update_slice(
-        jnp.zeros((2, NB, H), jnp.float32), bias_local, (0, 0, column)
-    )
+        [jnp.stack([layer[:, width : 2 * width], layer[:, 2 * width : 3 * width]]) for layer in layers]
+    )
+    grad_out = jnp.stack([layer[:, 3 * width :].T for layer in layers])
+    grad_up = jnp.stack([feed[:, :ffn] for feed in feeds])
+    grad_down = jnp.stack([feed[:, ffn:].T for feed in feeds])
+    gain_grads = gain_sums[:6] + jnp.stack(
+        [jnp.zeros_like(gain_c), jnp.zeros_like(gain_c), gain_c, gain_d, gain_e, jnp.zeros_like(gain_c)]
+    )
+    column = side * heads_local
+    bias_local = jnp.stack([near_table_grad(near_sums, far_sums), sums_c[4]])
+    bias_full = lax.dynamic_update_slice(jnp.zeros((2, NB, H), jnp.float32), bias_local, (0, 0, column))
     gain_total, bias_total = lax.psum((gain_grads, bias_full), ("dp", "wide", "narrow"))
     bias_grad = lax.dynamic_slice(bias_total, (0, 0, column), (2, NB, heads_local))
     return (
-        enc_final.astype(jnp.bfloat16),
+        enc_output,
         dec_final.astype(jnp.bfloat16),
         grad_enc,
         grad_dec,
-        tiles[0],
-        tiles[1],
-        tiles[2],
-        tiles[3],
-        tiles[4],
+        grad_query,
+        grad_kv,
+        grad_out,
+        grad_up,
+        grad_down,
         gain_total,
         bias_grad,
     )

time: 868 us -> 545 us (0.63)
  waiting for transfers between devices: 431 us -> 41.8 us
  Pallas kernels: 167 us -> 336 us
  local copies, waits for them, and re-layouts: 49.8 us -> 17 us
  matrix products: 92.4 us -> 61.3 us
  other arithmetic: 38.2 us -> 18.9 us
  between operations: 16.8 us -> 2.1 us
    reduce_scatter x3 -> x0, waiting for transfers between devices: 247 us -> none  [the longest x1 98.3 us: on_device(): lax.psum_scatter(grad_up.astype(jnp.bfloat16), 'wide', scatter_dimension=...]
    pallas_call x0 -> x2, Pallas kernels: none -> 193 us  [the longest x1 118 us: enc_backward(): pl.pallas_call(functools.partial(enc_backward_kernel, wide), in_specs=[vm...]
    unnamed x8 -> x0, waiting for transfers between devices: 98.3 us -> none
    ppermute x9 -> x6, waiting for transfers between devices: 55.8 us -> 16.3 us  [collect_rows(): lax.ppermute(lax.dynamic_slice_in_dim(parts, (1 - side) * half, half), 'n...]
    pallas_call x3 -> x2, Pallas kernels: 36.3 us -> 11.2 us  [attend_backward(): pl.pallas_call(functools.partial(attend_back_kernel, block, cols, steps,...]
    dot_general x14 -> x10, matrix products: 34.3 us -> 16.6 us  [dot_nt(): lax.dot_general(a, b, (((1,), (1,)), ((), ())), preferred_element_type=jn...]
    unnamed x271 -> x178, local copies, waits for them, and re-layouts: 24.7 us -> 8.46 us
    another operation x2 -> x6, local copies, waits for them, and re-layouts: 12.7 us -> 1.17 us  [the longest x2 0.93 us: on_device(): grad_out = jnp.stack([layer[:, 3 * width:].T for layer in layers])]
  transfers between devices with their start and end apart: 23 -> 13, of which waited for: 17 -> 9; matrix products, arithmetic and copies ran while one was open for 13% -> 9% of each run, Pallas kernels for 17% -> 46%
where the time goes in v2:
time: 545 us; the launch traced here: 535 us
  Pallas kernels  336 us (62%)
  matrix products  61.3 us (11%)
  blocking collectives  42.5 us (8%)
  waiting for transfers between devices  41.8 us (8%)
  other arithmetic  18.9 us (3%)
  local copies, waits for them, and re-layouts  17 us (3%)
  starting transfers between devices  15.9 us (3%)
    pallas_call x1, Pallas kernels, enc_forward(): pl.pallas_call(functools.partial(enc_forward_kernel, wide), in_specs=[vme...  120 us
    pallas_call x1, Pallas kernels, enc_backward(): pl.pallas_call(functools.partial(enc_backward_kernel, wide), in_specs=[vm...  118 us
    pallas_call x1, Pallas kernels, scatter_grads(): pl.pallas_call(functools.partial(scatter_kernel, wide, widths), in_specs=...  75.7 us
    psum x1, blocking collectives, on_device(): lax.psum((gain_grads, bias_full), ('dp', 'wide', 'narrow'))  42.5 us
    ppermute x6, waiting for transfers between devices, spread_rows(): other = lax.ppermute(own, 'narrow', swap)  25.5 us
    dot_general x10, matrix products, dot_tn(): lax.dot_general(a, b, (((0,), (0,)), ((), ())), preferred_element_type=jn...  17.4 us
    dot_general x10, matrix products, dot_nt(): lax.dot_general(a, b, (((1,), (1,)), ((), ())), preferred_element_type=jn...  16.6 us
    ppermute x6, waiting for transfers between devices, collect_rows(): lax.ppermute(lax.dynamic_slice_in_dim(parts, (1 - side) * half, half), 'n...  16.3 us
  transfers between devices with their start and end apart: 13, of which 9 were waited for; matrix products, arithmetic and copies ran while one was open for 9% of the time, Pallas kernels for 46%

profile of v2, /device:TPU:0, one launch (start us, length us, event | category | flops | bytes accessed | tf_op | source)
XLA Modules:
  0.0 535.0 jit_solution(11982848325577187645)
XLA Ops:
  3.8 3.0 collective-permute-start
  12.8 120.3 %shard_map.221 = (bf16[768,4608]{1,0:T(8,128)(2,1)}, bf16[768,6144]{1,0:T(8,128)(2,1)}, bf16[1024,768]{1,0:T(8,128)(2,1)}, bf16[1024,1152]{1,0:T(8,128)(2,1)}, b...) custom-call(bf16[512,768]{1,0:T(8,128)(2,1)} %x_own.3, ...), custom_call_target="tpu_custom_call" | custom-call | flops 10000000000 | bytes 60000000 | tf_op jit(solution)/shard_map/pallas_call | solution.py:690
  135.1 2.2 convolution_convert_fusion.18.refs_5_.refs_2_
  137.3 2.1 convolution_convert_fusion.19.refs_4_.refs_1_
  139.4 2.2 convolution_convert_fusion.20.refs_3_.refs_0_
  141.7 4.5 shard_map.222
  146.2 1.6 convolution_convert_fusion.14
  147.8 1.5 collective-permute-start.1
  149.3 2.9 convolution_convert_fusion.2.refs_4_.refs_2_
  152.2 2.2 collective-permute-done.1
  155.7 2.9 convolution_convert_fusion.3.refs_3_.refs_1_
  158.7 1.9 collective-permute-done.2
  161.2 2.1 convolution_convert_fusion.17.refs_2_.refs_0_
  163.3 6.1 %shard_map.223 = (bf16[6,256,1024]{2,1,0:T(8,128)(2,1)}, bf16[256,384]{1,0:T(8,128)(2,1)}, f32[256,384]{1,0:T(8,128)}) custom-call(s32[256,1]{1,0:T(8,128)} %copy.51.refs_0_, s32[1,1024]{1,0:T(1,128)} %bitcast.195, bf16[256,384]{1,0:T(8,128)(2,1)} %convolution_convert_fusion.17.refs_2_.refs_0_, bf16[1024,384]{1,0:T(8,128)(2,1)} %convolution_convert_fusion.3.refs_3_.refs_1_, ...), custom_call_target="tpu_custom_call" | custom-call | flops 805306368 | bytes 3145728 | tf_op jit(solution)/shard_map/pallas_call | solution.py:227
  169.5 1.6 convolution_convert_fusion.13
  174.0 4.9 collective-permute-done.3
  180.2 2.5 dynamic-slice_convert_fusion
  182.8 18.2 %collective-permute-done.4 = bf16[128,768]{1,0:T(8,128)(2,1)S(1)} collective-permute-done((bf16[128,768]{1,0:T(8,128)(2,1)S(1)}, bf16[128,768]{1,0:T(8,128)(2,1)S(1)}, u32[]{:S(2)}, u32[]{:S(2)}) %collective-permute-start.4) | collective-permute-done | bytes 196640 | tf_op jit(solution)/shard_map/ppermute | solution.py:1368
  200.9 2.5 fusion.9
  203.5 3.6 fusion.2
  209.1 5.6 %collective-permute-done.8 = bf16[128,768]{1,0:T(8,128)(2,1)S(1)} collective-permute-done((bf16[128,768]{1,0:T(8,128)(2,1)S(1)}, bf16[128,768]{1,0:T(8,128)(2,1)S(1)}, u32[]{:S(2)}, u32[]{:S(2)}) %collective-permute-start.8) | collective-permute-done | bytes 196640 | tf_op jit(solution)/shard_map/ppermute | solution.py:1374
  217.6 1.7 collective-permute-start.5
  219.3 1.8 collective-permute-done.9
  222.1 6.7 %shard_map.224 = (bf16[256,384]{1,0:T(8,128)(2,1)}, bf16[1024,384]{1,0:T(8,128)(2,1)}, bf16[1024,384]{1,0:T(8,128)(2,1)}) custom-call(bf16[256,384]{1,0:T(8,128)(2,1)} %convolution_convert_fusion.17.refs_2_.refs_0_, bf16[1024,384]{1,0:T(8,128)(2,1)} %convolution_convert_fusion.3.refs_3_.refs_1_, bf16[1024,384]{1,0:T(8,128)(2,1)} %convolution_convert_fusion.2.refs_4_.refs_2_, ...), custom_call_target="tpu_custom_call" | custom-call | flops 1610612736 | bytes 3145728 | tf_op jit(solution)/shard_map/pallas_call | solution.py:268
  228.8 2.4 fusion.35
  231.2 3.2 add_convert_fusion.memory_part
  234.5 117.7 %shard_map.225 = (f32[512,768]{1,0:T(8,128)}, bf16[96,4608]{1,0:T(8,128)(2,1)}, f32[8,768]{1,0:T(8,128)}, f32[6,8,1024]{2,1,0:T(8,128)}, f32[2,6,8,128]{3,2,1,0:T(8,128)}) custom-call(bf16[512,768]{1,0:T(8,128)(2,1)} %x_own.3, bf16[512,768]{1,0:T(8,128)(2,1)} %cot_own.1, bf16[512,768]{1,0:T(8,128)(2,1)} %collective-permute-done.6.cot_other, ...), custom_call_target="tpu_custom_call" | custom-call | flops 20000000000 | bytes 60000000 | tf_op jit(solution)/shard_map/pallas_call | solution.py:1229
  352.2 1.8 copy.78
  356.2 2.0 collective-permute-start.10
  359.2 1.5 reduce_sum.125
  360.7 1.6 fusion.28
  365.4 2.3 fusion.89
  367.7 1.7 collective-permute-start.11
  370.4 3.7 collective-permute-done.11
  374.1 2.2 convolution_convert_fusion.15.refs_6_
  376.3 4.5 shard_map.226
  380.8 1.6 fusion.44
  382.4 2.4 fusion.18
  390.2 1.8 fusion.13
  392.0 1.9 fusion.12
  395.2 2.3 fusion.1
  397.5 2.5 fusion.grad_in
  400.0 75.7 %shard_map.227 = bf16[96,6144]{1,0:T(8,128)(2,1)} custom-call(bf16[768,6144]{1,0:T(8,128)(2,1)} %fusion.grad_in), custom_call_target="tpu_custom_call" | custom-call | tf_op jit(solution)/shard_map/pallas_call | solution.py:1311
  475.7 1.5 convert_element_type.449
  478.7 1.5 convolution_add_fusion
  480.3 1.5 fusion.19
  486.9 2.1 collective-permute-done.12
  489.4 42.5 %all-reduce = (f32[6,768]{1,0:T(8,128)}, f32[2,32,12]{1,0,2:T(2,128)S(1)}) all-reduce(f32[6,768]{1,0:T(8,128)S(1)} %slice_add_fusion, f32[2,32,12]{1,0,2:T(2,128)S(1)} %copy_dynamic-update-slice_fusion), channel_id=1, replica_groups=mesh['dp'=2,'wide'=8,'narrow'=2] {'dp','wide','narrow'}, use_global_device_ids=true, to_apply=%region_13.14 | all-reduce | flops 5376 | bytes 43008 | tf_op jit(solution)/shard_map/psum | solution.py:1486
  (265 shorter events, 46.3 us)
Async XLA Ops:
  0.6 10.4 %copy-start.18 = (bf16[3,96,384]{2,1,0:T(8,128)(2,1)S(1)}, bf16[3,96,384]{2,1,0:T(8,128)(2,1)}, u32[]{:S(2)}) copy-start(bf16[3,96,384]{2,1,0:T(8,128)(2,1)} %param.18) | copy-start | bytes 663556
  0.7 10.4 %copy-start.16 = (bf16[3,2,96,384]{3,2,1,0:T(8,128)(2,1)S(1)}, bf16[3,2,96,384]{3,2,1,0:T(8,128)(2,1)}, u32[]{:S(2)}) copy-start(bf16[3,2,96,384]{3,2,1,0:T(8,128)(2,1)} %param.19) | copy-start | bytes 1327108
  0.7 10.4 %copy-start.19 = (bf16[3,384,96]{1,2,0:T(8,128)(2,1)S(1)}, bf16[3,384,96]{1,2,0:T(8,128)(2,1)}, u32[]{:S(2)}) copy-start(bf16[3,384,96]{1,2,0:T(8,128)(2,1)} %param.20) | copy-start | bytes 663556
  0.7 10.5 %copy-start.14 = (bf16[2,96,1536]{2,1,0:T(8,128)(2,1)S(1)}, bf16[2,96,1536]{2,1,0:T(8,128)(2,1)}, u32[]{:S(2)}) copy-start(bf16[2,96,1536]{2,1,0:T(8,128)(2,1)} %param.21) | copy-start | bytes 1769476
  1.5 9.7 %copy-start.41 = (f32[6,768]{1,0:T(8,128)}, f32[6,768]{1,0:T(8,128)S(1)}, u32[]{:S(2)}) copy-start(f32[6,768]{1,0:T(8,128)S(1)} %convert_element_type.385.gains) | copy-start | bytes 55300
  1.5 9.6 %copy-start.15 = (bf16[2,1536,96]{1,2,0:T(8,128)(2,1)S(1)}, bf16[2,1536,96]{1,2,0:T(8,128)(2,1)}, u32[]{:S(2)}) copy-start(bf16[2,1536,96]{1,2,0:T(8,128)(2,1)} %param.22) | copy-start | bytes 1769476
  3.8 135.7 %copy-start.30 = (bf16[128,768]{1,0:T(8,128)(2,1)}, bf16[128,768]{1,0:T(8,128)(2,1)S(1)}, u32[]{:S(2)}) copy-start(bf16[128,768]{1,0:T(8,128)(2,1)S(1)} %fusion.51) | copy-start | bytes 589828
  3.8 131.4 %collective-permute-start = (bf16[128,768]{1,0:T(8,128)(2,1)S(1)}, bf16[128,768]{1,0:T(8,128)(2,1)S(1)}, u32[]{:S(2)}, u32[]{:S(2)}) collective-permute-start(bf16[128,768]{1,0:T(8,128)(2,1)S(1)} %fusion.51), channel_id=1, source_target_pairs={{0,1},{1,0},{2,3},{3,2},{4,5},{5,4},{6,7},{7,6},{8,9},{9,8},{10,11... | collective-permute-start | bytes 589832 | tf_op jit(solution)/shard_map/ppermute | solution.py:1368
  12.8 120.3 %copy-start.39 = (s32[4096]{0:T(1024)}, s32[4096]{0:T(1024)S(1)}, u32[]{:S(2)}) copy-start(s32[4096]{0:T(1024)S(1)} %compare_select_fusion.2) | copy-start | bytes 49156
  12.8 121.2 %copy-start.68 = (s32[1,4]{1,0:T(1,128)S(1)}, s32[1,4]{1,0:T(1,128)}, u32[]{:S(2)}) copy-start(s32[1,4]{1,0:T(1,128)} %param.17) | copy-start | bytes 52
  134.3 5.1 copy-start.48
  135.1 4.3 copy-start.56
  139.4 9.9 %copy-start.69 = (bf16[1024,768]{1,0:T(8,128)(2,1)S(1)}, bf16[1024,768]{1,0:T(8,128)(2,1)}, u32[]{:S(2)}) copy-start(bf16[1024,768]{1,0:T(8,128)(2,1)} %get-tuple-element.45) | copy-start | bytes 4718596
  147.7 6.7 %copy-start = (bf16[128,768]{1,0:T(8,128)(2,1)S(1)}, bf16[128,768]{1,0:T(8,128)(2,1)}, u32[]{:S(2)}) copy-start(bf16[128,768]{1,0:T(8,128)(2,1)} %param.15) | copy-start | bytes 589828
  147.8 6.7 %collective-permute-start.1 = (bf16[128,768]{1,0:T(8,128)(2,1)S(1)}, bf16[128,768]{1,0:T(8,128)(2,1)S(1)}, u32[]{:S(2)}, u32[]{:S(2)}) collective-permute-start(bf16[128,768]{1,0:T(8,128)(2,1)S(1)} %constant_dynamic-slice_fusion.6), channel_id=1, source_target_pairs={{0,1},{1,0},{2,3},{3,2},{4,5},{5,4},{6,7},{7,6},{8,9},{9,8},{10,11... | collective-permute-start | bytes 589832 | tf_op jit(solution)/shard_map/ppermute | solution.py:1374
  154.7 5.8 %copy-start.33 = (bf16[128,768]{1,0:T(8,128)(2,1)}, bf16[128,768]{1,0:T(8,128)(2,1)S(1)}, u32[]{:S(2)}) copy-start(bf16[128,768]{1,0:T(8,128)(2,1)S(1)} %multiply_convert_fusion.2) | copy-start | bytes 589828
  154.8 5.8 %collective-permute-start.2 = (bf16[128,768]{1,0:T(8,128)(2,1)S(1)}, bf16[128,768]{1,0:T(8,128)(2,1)S(1)}, u32[]{:S(2)}, u32[]{:S(2)}) collective-permute-start(bf16[128,768]{1,0:T(8,128)(2,1)S(1)} %multiply_convert_fusion.2), channel_id=1, source_target_pairs={{0,1},{1,0},{2,3},{3,2},{4,5},{5,4},{6,7},{7,6},{8,9},{9,8},{10,11... | collective-permute-start | bytes 589832 | tf_op jit(solution)/shard_map/ppermute | solution.py:1368
  163.3 8.7 %copy-start.7 = (bf16[128,768]{1,0:T(8,128)(2,1)S(1)}, bf16[128,768]{1,0:T(8,128)(2,1)}, u32[]{:S(2)}) copy-start(bf16[128,768]{1,0:T(8,128)(2,1)} %param.26) | copy-start | bytes 589828
  163.3 9.8 %copy-start.55 = (bf16[512,768]{1,0:T(8,128)(2,1)S(1)}, bf16[512,768]{1,0:T(8,128)(2,1)}, u32[]{:S(2)}) copy-start(bf16[512,768]{1,0:T(8,128)(2,1)} %cot_own.1) | copy-start | bytes 2359300
  171.1 7.9 %collective-permute-start.3 = (bf16[128,768]{1,0:T(8,128)(2,1)S(1)}, bf16[128,768]{1,0:T(8,128)(2,1)S(1)}, u32[]{:S(2)}, u32[]{:S(2)}) collective-permute-start(bf16[128,768]{1,0:T(8,128)(2,1)S(1)} %constant_dynamic-slice_fusion.5), channel_id=1, source_target_pairs={{0,1},{1,0},{2,3},{3,2},{4,5},{5,4},{6,7},{7,6},{8,9},{9,8},{10,11... | collective-permute-start | bytes 589832 | tf_op jit(solution)/shard_map/ppermute | solution.py:1374
  172.0 31.5 %collective-permute-start.7 = (bf16[128,768]{1,0:T(8,128)(2,1)S(1)}, bf16[128,768]{1,0:T(8,128)(2,1)S(1)}, u32[]{:S(2)}, u32[]{:S(2)}) collective-permute-start(bf16[128,768]{1,0:T(8,128)(2,1)S(1)} %copy-done.7), channel_id=1, source_target_pairs={{0,1},{1,0},{2,3},{3,2},{4,5},{5,4},{6,7},{7,6},{8,9},{9,8},{10,11... | collective-permute-start | bytes 589832 | tf_op jit(solution)/shard_map/ppermute | solution.py:1368
  173.2 61.3 %collective-permute-start.6 = (bf16[512,768]{1,0:T(8,128)(2,1)S(1)}, bf16[512,768]{1,0:T(8,128)(2,1)}, u32[]{:S(2)}, u32[]{:S(2)}) collective-permute-start(bf16[512,768]{1,0:T(8,128)(2,1)S(1)} %copy-done.55), channel_id=1, source_target_pairs={{0,1},{1,0},{2,3},{3,2},{4,5},{5,4},{6,7},{7,6},{8,9},{9,8},{10,11... | collective-permute-start | bytes 2359304 | tf_op jit(solution)/shard_map/ppermute | solution.py:1386
  179.2 35.7 %copy-start.44 = (f32[128]{0:T(128)}, f32[128]{0:T(128)S(1)}, u32[]{:S(2)}) copy-start(f32[128]{0:T(128)S(1)} %fusion.77) | copy-start | bytes 1540
  179.3 24.2 %copy-start.35 = (bf16[128,768]{1,0:T(8,128)(2,1)}, bf16[128,768]{1,0:T(8,128)(2,1)S(1)}, u32[]{:S(2)}) copy-start(bf16[128,768]{1,0:T(8,128)(2,1)S(1)} %multiply_convert_fusion.1) | copy-start | bytes 589828
  179.3 21.7 %collective-permute-start.4 = (bf16[128,768]{1,0:T(8,128)(2,1)S(1)}, bf16[128,768]{1,0:T(8,128)(2,1)S(1)}, u32[]{:S(2)}, u32[]{:S(2)}) collective-permute-start(bf16[128,768]{1,0:T(8,128)(2,1)S(1)} %multiply_convert_fusion.1), channel_id=1, source_target_pairs={{0,1},{1,0},{2,3},{3,2},{4,5},{5,4},{6,7},{7,6},{8,9},{9,8},{10,11... | collective-permute-start | bytes 589832 | tf_op jit(solution)/shard_map/ppermute | solution.py:1368
  180.2 26.9 %slice-start = ((s8[9437184]{0:T(1024)(128)(4,1)}), s8[4194304]{0:T(1024)(128)(4,1)S(1)}, s32[]{:S(2)}) async-start(s8[9437184]{0:T(1024)(128)(4,1)} %bitcast.181), calls=%async_computation | async-start | bytes 8388608
  182.8 24.4 %slice-start.1 = ((s8[9437184]{0:T(1024)(128)(4,1)}), s8[4194304]{0:T(1024)(128)(4,1)S(1)}, s32[]{:S(2)}) async-start(s8[9437184]{0:T(1024)(128)(4,1)} %bitcast.181), calls=%async_computation.1 | async-start | bytes 8388608
  203.5 12.3 %copy-start.71 = (f32[256,1536]{1,0:T(8,128)}, f32[256,1536]{1,0:T(8,128)S(1)}, u32[]{:S(2)}) copy-start(f32[256,1536]{1,0:T(8,128)S(1)} %fusion.9) | copy-start | bytes 4718596
  208.0 6.8 %copy-start.2 = (bf16[256,768]{1,0:T(8,128)(2,1)}, bf16[256,768]{1,0:T(8,128)(2,1)S(1)}, u32[]{:S(2)}) copy-start(bf16[256,768]{1,0:T(8,128)(2,1)S(1)} %fusion.20) | copy-start | bytes 1179652
  208.1 6.6 %collective-permute-start.8 = (bf16[128,768]{1,0:T(8,128)(2,1)S(1)}, bf16[128,768]{1,0:T(8,128)(2,1)S(1)}, u32[]{:S(2)}, u32[]{:S(2)}) collective-permute-start(bf16[128,768]{1,0:T(8,128)(2,1)S(1)} %constant_dynamic-slice_fusion.3), channel_id=1, source_target_pairs={{0,1},{1,0},{2,3},{3,2},{4,5},{5,4},{6,7},{7,6},{8,9},{9,8},{10,11... | collective-permute-start | bytes 589832 | tf_op jit(solution)/shard_map/ppermute | solution.py:1374
  215.4 5.7 %copy-start.21 = (bf16[128,768]{1,0:T(8,128)(2,1)}, bf16[128,768]{1,0:T(8,128)(2,1)S(1)}, u32[]{:S(2)}) copy-start(bf16[128,768]{1,0:T(8,128)(2,1)S(1)} %fusion.88) | copy-start | bytes 589828
  215.4 5.7 %collective-permute-start.9 = (bf16[128,768]{1,0:T(8,128)(2,1)S(1)}, bf16[128,768]{1,0:T(8,128)(2,1)S(1)}, u32[]{:S(2)}, u32[]{:S(2)}) collective-permute-start(bf16[128,768]{1,0:T(8,128)(2,1)S(1)} %fusion.88), channel_id=1, source_target_pairs={{0,1},{1,0},{2,3},{3,2},{4,5},{5,4},{6,7},{7,6},{8,9},{9,8},{10,11... | collective-permute-start | bytes 589832 | tf_op jit(solution)/shard_map/ppermute | solution.py:1368
  216.9 14.3 %copy-start.17 = (bf16[256,768]{1,0:T(8,128)(2,1)}, bf16[256,768]{1,0:T(8,128)(2,1)S(1)}, u32[]{:S(2)}) copy-start(bf16[256,768]{1,0:T(8,128)(2,1)S(1)} %fusion.23) | copy-start | bytes 1179652
  217.6 147.7 %collective-permute-start.5 = (bf16[128,768]{1,0:T(8,128)(2,1)}, bf16[128,768]{1,0:T(8,128)(2,1)}, u32[]{:S(2)}, u32[]{:S(2)}) collective-permute-start(bf16[128,768]{1,0:T(8,128)(2,1)} %constant_dynamic-slice_fusion.4), channel_id=1, source_target_pairs={{0,1},{1,0},{2,3},{3,2},{4,5},{5,4},{6,7},{7,6},{8,9},{9,8},{10,11... | collective-permute-start | bytes 589832 | tf_op jit(solution)/shard_map/ppermute | solution.py:1374
  221.1 7.7 %copy-start.64 = (bf16[128,768]{1,0:T(8,128)(2,1)}, bf16[128,768]{1,0:T(8,128)(2,1)S(1)}, u32[]{:S(2)}) copy-start(bf16[128,768]{1,0:T(8,128)(2,1)S(1)} %collective-permute-done.9) | copy-start | bytes 589828
  234.5 119.5 %copy-start.23 = (bf16[256,384]{1,0:T(8,128)(2,1)S(1)}, bf16[256,384]{1,0:T(8,128)(2,1)}, u32[]{:S(2)}) copy-start(bf16[256,384]{1,0:T(8,128)(2,1)} %get-tuple-element.62) | copy-start | bytes 589828
  352.2 6.0 %copy-start.4 = (bf16[96,4608]{1,0:T(8,128)(2,1)S(1)}, bf16[96,4608]{1,0:T(8,128)(2,1)}, u32[]{:S(2)}) copy-start(bf16[96,4608]{1,0:T(8,128)(2,1)} %get-tuple-element.68) | copy-start | bytes 2654212
  356.2 7.5 %collective-permute-start.10 = (bf16[128,768]{1,0:T(8,128)(2,1)}, bf16[128,768]{1,0:T(8,128)(2,1)}, u32[]{:S(2)}, u32[]{:S(2)}) collective-permute-start(bf16[128,768]{1,0:T(8,128)(2,1)} %constant_dynamic-slice_fusion.2), channel_id=1, source_target_pairs={{0,1},{1,0},{2,3},{3,2},{4,5},{5,4},{6,7},{7,6},{8,9},{9,8},{10,11... | collective-permute-start | bytes 589832 | tf_op jit(solution)/shard_map/ppermute | solution.py:1374
  360.6 8.8 %copy-start.51 = (f32[2,6]{1,0:T(2,128)S(1)}, f32[2,6]{1,0:T(2,128)}, u32[]{:S(2)}) copy-start(f32[2,6]{1,0:T(2,128)} %reduce_sum.125) | copy-start | bytes 148
  360.6 9.6 %copy-start.12 = (f32[1,96,384]{2,1,0:T(8,128)S(1)}, f32[1,96,384]{2,1,0:T(8,128)}, u32[]{:S(2)}) copy-start(f32[1,96,384]{2,1,0:T(8,128)} %get-tuple-element.103) | copy-start | bytes 442372
  360.6 9.7 %copy-start.13 = (f32[1,96,384]{2,1,0:T(8,128)S(1)}, f32[1,96,384]{2,1,0:T(8,128)}, u32[]{:S(2)}) copy-start(f32[1,96,384]{2,1,0:T(8,128)} %get-tuple-element.104) | copy-start | bytes 442372
  367.7 6.4 %copy-start.27 = (bf16[128,768]{1,0:T(8,128)(2,1)}, bf16[128,768]{1,0:T(8,128)(2,1)S(1)}, u32[]{:S(2)}) copy-start(bf16[128,768]{1,0:T(8,128)(2,1)S(1)} %get-tuple-element.84) | copy-start | bytes 589828
  367.7 6.4 %collective-permute-start.11 = (bf16[128,768]{1,0:T(8,128)(2,1)S(1)}, bf16[128,768]{1,0:T(8,128)(2,1)S(1)}, u32[]{:S(2)}, u32[]{:S(2)}) collective-permute-start(bf16[128,768]{1,0:T(8,128)(2,1)S(1)} %get-tuple-element.84), channel_id=1, source_target_pairs={{0,1},{1,0},{2,3},{3,2},{4,5},{5,4},{6,7},{7,6},{8,9},{9,8},{10,11... | collective-permute-start | bytes 589832 | tf_op jit(solution)/shard_map/ppermute | solution.py:1368
  376.3 6.1 %copy-start.31 = (bf16[128,768]{1,0:T(8,128)(2,1)S(1)}, bf16[128,768]{1,0:T(8,128)(2,1)}, u32[]{:S(2)}) copy-start(bf16[128,768]{1,0:T(8,128)(2,1)} %copy-done.30) | copy-start | bytes 589828
  481.8 7.3 %collective-permute-start.12 = (bf16[128,768]{1,0:T(8,128)(2,1)S(1)}, bf16[128,768]{1,0:T(8,128)(2,1)S(1)}, u32[]{:S(2)}, u32[]{:S(2)}) collective-permute-start(bf16[128,768]{1,0:T(8,128)(2,1)S(1)} %constant_dynamic-slice_fusion.1), channel_id=1, source_target_pairs={{0,1},{1,0},{2,3},{3,2},{4,5},{5,4},{6,7},{7,6},{8,9},{9,8},{10,11... | collective-permute-start | bytes 589832 | tf_op jit(solution)/shard_map/ppermute | solution.py:1374
  485.1 47.4 %copy-start.53 = (f32[128]{0:T(128)S(1)}, f32[128]{0:T(128)}, u32[]{:S(2)}) copy-start(f32[128]{0:T(128)} %copy-done.52) | copy-start | bytes 1540
  485.1 47.4 %copy-start.3 = (f32[128,768]{1,0:T(8,128)S(1)}, f32[128,768]{1,0:T(8,128)}, u32[]{:S(2)}) copy-start(f32[128,768]{1,0:T(8,128)} %get-tuple-element.85) | copy-start | bytes 1179652
  485.1 48.2 %copy-start.1 = (f32[512,768]{1,0:T(8,128)S(1)}, f32[512,768]{1,0:T(8,128)}, u32[]{:S(2)}) copy-start(f32[512,768]{1,0:T(8,128)} %get-tuple-element.128) | copy-start | bytes 4718596
  (43 other events, 103.0 us)
